TPU v7x, 32 devices: a whole 2x2x4 slice. The times are simulated.
32 devices in a mesh: seqhi: 4 (over x, core), seqlo: 8 (over z, y).
Axes of the slice: x: 2, y: 2, z: 4, core: 2. Of those that a mesh axis runs over, the one named last changes fastest.
Arguments:
- queries: float32 [4096, 768], P(('seqhi', 'seqlo')), may hold values from -6 to 6
- keys: float32 [4096, 768], P(('seqhi', 'seqlo')), may hold values from -6 to 6
- values: float32 [4096, 768], P(('seqhi', 'seqlo')), may hold values from -6 to 6
- cotangent: float32 [4096, 768], P(('seqhi', 'seqlo')), may hold values from -6 to 6
Outputs:
- attended: float32 [4096, 768], P(('seqhi', 'seqlo'))
- query_grad: float32 [4096, 768], P(('seqhi', 'seqlo'))
- key_grad: float32 [4096, 768], P(('seqhi', 'seqlo'))
- value_grad: float32 [4096, 768], P(('seqhi', 'seqlo'))
All inputs are finite; a program needn't handle non-finite values.
Results may differ from a plain program's by a relative error of at most 0.0003.
Values sent between devices are 32-bit elements; how exact they have to be, the bound alone decides.
No kernel may reach another device: no remote copies, remote signals or barrier semaphores. Data moves between devices by JAX's collectives and lax.ppermute only.
A program may use at most 128 MiB of HBM per device.

v0:
```python
import math

import jax
import jax.numpy as jnp
from jax import lax
from jax.experimental import pallas as pl
from jax.experimental.pallas import tpu as pltpu
from jax.sharding import PartitionSpec as P

HEADS = 12
BLOCK = 128
HEAD_DIM = 64
LANES = 2 * HEAD_DIM
AXES = ("seqhi", "seqlo")
VMEM_LIMIT = 20 * 1024 * 1024
F32 = jnp.float32
BF16 = jnp.bfloat16
LOG2_E = 1.0 / math.log(2.0)
SCALE = 1.0 / math.sqrt(HEAD_DIM)


def struct(*shape):
    return jax.ShapeDtypeStruct(shape, F32)


def call(kernel, operands, outs, scratch=(), scalar=None, flops=0, exps=0, where=None):
    vmem = pl.BlockSpec(memory_space=pltpu.VMEM)
    smem = pl.BlockSpec(memory_space=pltpu.SMEM)
    in_specs = [pl.BlockSpec(memory_space=where) if where else vmem] * len(operands)
    if scalar is not None:
        operands = [scalar, *operands]
        in_specs = [smem, *in_specs]
    moved = sum(4 * math.prod(a.shape) for a in [*operands, *outs])
    return pl.pallas_call(
        kernel,
        out_shape=list(outs),
        in_specs=in_specs,
        out_specs=[vmem] * len(outs),
        scratch_shapes=list(scratch),
        compiler_params=pltpu.CompilerParams(vmem_limit_bytes=VMEM_LIMIT),
        cost_estimate=pl.CostEstimate(
            flops=flops, bytes_accessed=moved, transcendentals=exps
        ),
    )(*operands)


def exchange(value, offset):
    count = lax.axis_size(AXES)
    return lax.ppermute(value, AXES, [(i, i ^ offset) for i in range(count)])


def ordered(value, after):
    return value if after is None else lax.optimization_barrier((value, after))[0]


def half_difference(ref, lead, first, count):
    even = ref[(*lead, pl.ds(first, count, stride=2), slice(None))]
    odd = ref[(*lead, pl.ds(first + 1, count, stride=2), slice(None))]
    return 0.5 * (even - odd)


def put_pairs(ref, lead, total, difference):
    count = total.shape[0]
    ref[(*lead, pl.ds(0, count, stride=2), slice(None))] = total + difference
    ref[(*lead, pl.ds(1, count, stride=2), slice(None))] = total - difference


def mean_rows(ref, lead, first, count, factor):
    total = None
    for step in range(factor):
        rows = pl.ds(first + step, count, stride=factor)
        part = ref[(*lead, rows, slice(None))]
        total = part if total is None else total + part
    return total * (1.0 / factor)


def add_spread(ref, lead, first, value, factor):
    count = value.shape[0]
    value = value * (1.0 / factor)
    for step in range(factor):
        rows = pl.ds(first + step, count, stride=factor)
        place = (*lead, rows, slice(None))
        ref[place] = ref[place] + value


class Tree:
    def __init__(self, first_bit, own_rows):
        self.bits = bits = len(own_rows)
        self.first_bit = first_bit
        self.own_rows = own_rows
        self.held = {}
        self.payload = {}
        for step in range(bits - 1, -1, -1):
            rows = self.own_rows[step]
            payload = []
            fresh = {step: [(step, 0, rows)] if rows else []}
            for level in range(step + 1, bits):
                for piece in self.held[level]:
                    payload.append(piece)
                    fresh.setdefault(level, []).append((step, rows, piece[2]))
                    rows += piece[2]
            self.payload[step] = payload
            for level, pieces in fresh.items():
                self.held[level] = self.held.get(level, []) + pieces

    def rows(self, step):
        return self.own_rows[step] + sum(piece[2] for piece in self.payload[step])

    def partner(self, value, step):
        return exchange(value, 1 << self.first_bit + step)

    def gather(self, own, after=None):
        arrived = [None] * self.bits
        for step in range(self.bits - 1, -1, -1):
            parts = [own[step]] if self.own_rows[step] else []
            for source, row, rows in self.payload[step]:
                part = arrived[source]
                whole = rows == part.shape[1]
                parts.append(part if whole else part[:, row : row + rows])
            sent = jnp.concatenate(parts, axis=1) if len(parts) > 1 else parts[0]
            if step == 0:
                sent = ordered(sent, after)
            arrived[step] = self.partner(sent, step)
        return arrived

    def scatter(self, grads, front=None):
        grads = list(grads)
        returned = []
        for step in range(self.bits):
            sent = grads[step]
            if step == 0 and front is not None:
                rows = front.shape[1]
                back = self.partner(jnp.concatenate([front, sent], axis=1), step)
                front, back = back[:, :rows], back[:, rows:]
            else:
                back = self.partner(sent, step)
            returned.append(back)
            filled = self.own_rows[step]
            for source, row, rows in self.payload[step]:
                part = back[:, filled : filled + rows]
                grads[source] = grads[source].at[:, row : row + rows].add(part)
                filled += rows
        return returned if front is None else (returned, front)


def split(value):
    high = value.astype(BF16).astype(F32)
    return high, value - high


def halves_by_head(value):
    high, low = split(value)
    first = lax.broadcasted_iota(jnp.int32, value.shape, 1) < HEAD_DIM
    one = jnp.where(first, high, pltpu.roll(low, HEAD_DIM, 1))
    two = jnp.where(first, pltpu.roll(high, HEAD_DIM, 1), low)
    return one, two


def dot(lhs, rhs, dims):
    return lax.dot_general(lhs, rhs, (dims, ((), ())), preferred_element_type=F32)


NN = ((1,), (0,))
NT = ((1,), (1,))


BOTH = 2 * BLOCK
GROUP = 3


def halves_of(sets, ins, which, pairs, pair):
    tile = which * pairs + pair
    parts = [ins[index][tile, pl.ds(row, rows), :] for _, index, row, rows in sets]
    return halves_by_head(jnp.concatenate(parts, axis=0))


def segment_levels(sets):
    levels, filled = [], 0
    for level, _, _, rows in sets:
        if filled % BLOCK == 0:
            levels.append(level)
        filled += rows
    return levels


def four_rows(value):
    high, low = split(value)
    four = jnp.concatenate([high, high, low, low], axis=0).astype(BF16)
    return four, jnp.concatenate([high, low], axis=0).astype(BF16)


def store_split(ref, lead, rows, value):
    high = value.astype(BF16)
    ref[(lead, 0, rows)] = high
    ref[(lead, 1, rows)] = (value - high.astype(F32)).astype(BF16)


def fold_rows(value):
    return value[:HEAD_DIM] + value[HEAD_DIM:]


def fold_heads(one, two):
    first = lax.broadcasted_iota(jnp.int32, one.shape, 1) < HEAD_DIM
    return jnp.where(
        first, one + pltpu.roll(one, HEAD_DIM, 1), two + pltpu.roll(two, HEAD_DIM, 1)
    )


def twice(value):
    return jnp.concatenate([value, value], axis=1)


def stacked(ref, at, rows=slice(None)):
    return jnp.concatenate([ref[at, 0, rows], ref[at, 1, rows]], axis=0)


def abreast(ref, at, rows=slice(None)):
    return jnp.concatenate([ref[at, 0, rows], ref[at, 1, rows]], axis=1)


def column_scores(levels, keys, at, q_four, s_ref):
    highest = None
    for index, level in enumerate(levels):
        rows = pl.ds(index * BLOCK, BLOCK)
        s = dot(twice(keys[at, rows]), q_four, NN)
        s = s + float(level) if level else s
        s_ref[at, rows] = s
        top = jnp.max(s.reshape(BLOCK // 8, 8, BOTH), axis=0)
        highest = top if highest is None else jnp.maximum(highest, top)
    return jnp.max(highest, axis=0, keepdims=True)


def exponents(levels, at, top, s_ref, e_ref, keep):
    summed = None
    for index in range(len(levels)):
        rows = pl.ds(index * BLOCK, BLOCK)
        e = jnp.exp2(s_ref[at, rows] - top)
        if keep:
            s_ref[at, rows] = e
        store_split(e_ref, at, rows, e)
        part = jnp.sum(e.reshape(BLOCK // 8, 8, BOTH), axis=0)
        summed = part if summed is None else summed + part
    return jnp.sum(summed, axis=0, keepdims=True)


def head_rows(ref, pair, head):
    return ref[pair, pl.ds(head * HEAD_DIM, HEAD_DIM)]


def each_group(pairs, body):
    for first in range(0, pairs, GROUP):
        group = range(first, min(first + GROUP, pairs))
        body(group, [(pair, head, 2 * pair + head) for pair in group for head in (0, 1)])


def costs(pairs, rows, products, exps=0):
    return dict(
        flops=2 * 4 * products * pairs * 2 * rows * BOTH * HEAD_DIM,
        exps=exps * pairs * 2 * rows * BOTH,
    )


def put_halves(pairs, sets, ins, group, plain, turned):
    for which in range(2):
        for pair in group:
            for head, value in enumerate(halves_of(sets, ins, which, pairs, pair)):
                plain[which][2 * pair + head] = value.astype(BF16)
                turned[which][2 * pair + head] = value.T.astype(BF16)


def attend_first(pairs, sets, operands, turned):
    total = sum(s[3] for s in sets)
    levels = segment_levels(sets)

    def kernel(turn_in, *refs):
        ins = refs[: len(operands)]
        kt, vc, e_ref, tops, sums, out, s_ref, kc, vt = refs[len(operands) :]

        def body(group, heads):
            put_halves(pairs, sets, ins, group, (kc, vc), (kt, vt))
            for pair, head, at in heads:
                q_four, _ = four_rows(head_rows(turn_in, pair, head))
                tops[at] = column_scores(levels, kc, at, q_four, s_ref)
            for _, _, at in heads:
                sums[at] = exponents(levels, at, tops[at], s_ref, e_ref, False)
            for _, _, at in heads:
                out[at] = fold_rows(dot(twice(vt[at]), stacked(e_ref, at), NN))

        each_group(pairs, body)

    heads = 2 * pairs
    outs = [
        jax.ShapeDtypeStruct((heads, LANES, total), BF16),
        jax.ShapeDtypeStruct((heads, total, LANES), BF16),
        jax.ShapeDtypeStruct((heads, 2, total, BOTH), BF16),
    ]
    outs += [struct(heads, 1, BOTH)] * 2 + [struct(heads, HEAD_DIM, BOTH)]
    return call(
        kernel,
        [turned, *operands],
        outs,
        scratch=[
            pltpu.VMEM((heads, total, BOTH), F32),
            pltpu.VMEM((heads, total, LANES), BF16),
            pltpu.VMEM((heads, LANES, total), BF16),
        ],
        **costs(pairs, total, 2, 1),
    )


def attend_last(pairs, sets, operands, turned, tops, sums, partial):
    total = sum(s[3] for s in sets)
    levels = segment_levels(sets)

    def kernel(turn_in, top_in, sum_in, part_in, *refs):
        ins = refs[: len(operands)]
        grads = refs[len(operands) : 2 * len(operands)]
        o_keep, o_send, g_out, r_out, dq_out = refs[2 * len(operands) : -7]
        s_ref, e_ref, d_ref, kc, vc, kt, vt = refs[-7:]

        def body(group, heads):
            put_halves(pairs, sets, ins, group, (kc, vc), (kt, vt))
            queries = {}
            top = {}
            for pair, head, at in heads:
                q_four, queries[at] = four_rows(head_rows(turn_in, pair, head))
                top[at] = column_scores(levels, kc, at, q_four, s_ref)
            inverse = {}
            rescale = {}
            for _, _, at in heads:
                first_top = top_in[at]
                highest = jnp.maximum(top[at], first_top)
                rescale[at] = jnp.exp2(first_top - highest)
                summed = exponents(levels, at, highest, s_ref, e_ref, True)
                inverse[at] = 1.0 / (summed + sum_in[at] * rescale[at])
            output = {}
            cotangents = {}
            row_dot = {}
            for pair, head, at in heads:
                o = fold_rows(dot(twice(vt[at]), stacked(e_ref, at), NN))
                o = (o + part_in[at] * rescale[at]) * inverse[at]
                output[at] = o
                scaled = head_rows(turn_in, pairs + pair, head) * inverse[at]
                cotangents[at] = four_rows(scaled)
                row_dot[at] = jnp.sum(o * scaled, axis=0, keepdims=True)
                g_out[at] = scaled * rescale[at]
                r_out[at] = row_dot[at] * rescale[at]
            for _, _, at in heads:
                for index in range(len(levels)):
                    rows = pl.ds(index * BLOCK, BLOCK)
                    dp = dot(twice(vc[at, rows]), cotangents[at][0], NN)
                    store_split(d_ref, at, rows, s_ref[at, rows] * (dp - row_dot[at]))
            key_grads = {}
            value_grads = {}
            for _, _, at in heads:
                value_grads[at] = dot(abreast(e_ref, at), twice(cotangents[at][1]), NT)
                key_grads[at] = dot(abreast(d_ref, at), twice(queries[at]), NT)
                dq_out[at] = fold_rows(dot(twice(kt[at]), stacked(d_ref, at), NN))
            for pair in group:
                put_grads(pairs, pair, sets, grads, key_grads, value_grads)
                both = [output[2 * pair], output[2 * pair + 1]]
                both = jnp.concatenate(both, axis=0).T
                o_keep[pair] = both[:BLOCK]
                o_send[pair] = both[BLOCK:]

        each_group(pairs, body)

    heads = 2 * pairs
    outs = [struct(*a.shape) for a in operands]
    outs += [struct(pairs, BLOCK, LANES)] * 2
    outs += [struct(heads, HEAD_DIM, BOTH), struct(heads, 1, BOTH)]
    outs.append(struct(heads, HEAD_DIM, BOTH))
    return call(
        kernel,
        [turned, tops, sums, partial, *operands],
        outs,
        scratch=[pltpu.VMEM((heads, total, BOTH), F32)]
        + [pltpu.VMEM((heads, 2, total, BOTH), BF16)] * 2
        + [pltpu.VMEM((heads, total, LANES), BF16)] * 2
        + [pltpu.VMEM((heads, LANES, total), BF16)] * 2,
        **costs(pairs, total, 6, 1),
    )


def put_grads(pairs, pair, sets, grads, key_grads, value_grads):
    for which, parts in enumerate((key_grads, value_grads)):
        both = fold_heads(parts[2 * pair], parts[2 * pair + 1])
        if which == 0:
            both = both * (1.0 / LOG2_E)
        filled = 0
        for _, index, row, rows in sets:
            piece = both[filled : filled + rows]
            grads[index][which * pairs + pair, pl.ds(row, rows), :] = piece
            filled += rows


def attend_back(pairs, sets, shapes, first, kept, turned, g_scaled, row_dot, dq, last):
    total = sum(s[3] for s in sets)
    segments = total // BLOCK

    def kernel(turn_in, kt, vc, e_ref, g_in, r_in, dq_in, *refs):
        grads = refs[: len(shapes)]
        dq_out = refs[len(shapes) : -1]
        d_ref = refs[-1]
        span = pl.ds(first, total)

        def body(group, heads):
            cotangents = {}
            for _, _, at in heads:
                g_four, cotangents[at] = four_rows(g_in[at])
                for index in range(segments):
                    rows = pl.ds(first + index * BLOCK, BLOCK)
                    dp = dot(twice(vc[at, rows]), g_four, NN)
                    e = e_ref[at, 0, rows].astype(F32) + e_ref[at, 1, rows].astype(F32)
                    place = pl.ds(index * BLOCK, BLOCK)
                    store_split(d_ref, at, place, e * (dp - r_in[at]))
            queries_grad = {}
            key_grads = {}
            value_grads = {}
            for pair, head, at in heads:
                _, q_rows = four_rows(head_rows(turn_in, pair, head))
                g_rows = cotangents[at]
                value_grads[at] = dot(abreast(e_ref, at, span), twice(g_rows), NT)
                key_grads[at] = dot(abreast(d_ref, at), twice(q_rows), NT)
                part = dot(twice(kt[at, :, span]), stacked(d_ref, at), NN)
                queries_grad[at] = fold_rows(part) + dq_in[at]
            for pair in group:
                put_grads(pairs, pair, sets, grads, key_grads, value_grads)
                both = [queries_grad[2 * pair], queries_grad[2 * pair + 1]]
                if last:
                    both = jnp.concatenate(both, axis=0).T * SCALE
                    dq_out[0][pair] = both[:BLOCK]
                    dq_out[1][pair] = both[BLOCK:]
                else:
                    for head in range(2):
                        dq_out[0][2 * pair + head] = both[head]

        each_group(pairs, body)

    outs = [struct(*shape) for shape in shapes]
    if last:
        outs += [struct(pairs, BLOCK, LANES)] * 2
    else:
        outs.append(struct(*dq.shape))
    return call(
        kernel,
        [turned, *kept, g_scaled, row_dot, dq],
        outs,
        scratch=[pltpu.VMEM((2 * pairs, 2, total, BOTH), BF16)],
        **costs(pairs, total, 4),
    )


def copy_columns(moves, ins, sems, bit):
    started = []
    for operand, theirs, column, place in moves:
        side = 1 - bit if theirs else bit
        column = side * (ins[operand].shape[1] // 2) + column
        column = pl.ds(pl.multiple_of(column, LANES), LANES)
        copy = pltpu.make_async_copy(
            ins[operand].at[:, column], place, sems.at[len(started)]
        )
        copy.start()
        started.append(copy)
    return started


def pack(pairs, first, second, scalar):
    def kernel(bit, one, two, theirs, mine, sems):
        moves = []
        for tile in range(2 * pairs):
            for out, other in ((theirs, True), (mine, False)):
                column = tile % pairs * LANES
                moves.append((tile // pairs, other, column, out.at[tile]))
        for copy in copy_columns(moves, (one, two), sems, bit[0]):
            copy.wait()

    return call(
        kernel,
        [first, second],
        [struct(2 * pairs, BLOCK, LANES)] * 2,
        scratch=[pltpu.SemaphoreType.DMA((4 * pairs,))],
        scalar=scalar,
        where=pl.ANY,
    )


QUARTER = BLOCK // 4
HALF = BLOCK // 2


def pack_coarse(pairs, keys, values, scalar):
    def kernel(bit, k, v, mine, f_theirs, f_mine, c_theirs, c_mine, rest, theirs, sems):
        moves = []
        for out, other in ((theirs, True), (mine, False)):
            for tile in range(2 * pairs):
                column = tile % pairs * LANES
                moves.append((tile // pairs, other, column, out.at[tile]))
        copies = copy_columns(moves, (k, v), sems, bit[0])
        for index, copy in enumerate(copies):
            copy.wait()
            tile = index % (2 * pairs)
            other = index < 2 * pairs
            source, finest, coarse = (
                (theirs, f_theirs, c_theirs) if other else (mine, f_mine, c_mine)
            )
            finest[tile] = mean_rows(source, (tile,), 0, HALF, 2)
            coarse[tile] = mean_rows(finest, (tile,), 0, QUARTER, 2)
            if other:
                rest[tile, :QUARTER] = half_difference(finest, (tile,), 0, QUARTER)
                rest[tile, QUARTER:] = half_difference(source, (tile,), 0, HALF)

    return call(
        kernel,
        [keys, values],
        [struct(2 * pairs, BLOCK, LANES)]
        + [struct(2 * pairs, HALF, LANES)] * 2
        + [struct(2 * pairs, QUARTER, LANES)] * 2
        + [struct(2 * pairs, QUARTER + HALF, LANES)],
        scratch=[
            pltpu.VMEM((2 * pairs, BLOCK, LANES), F32),
            pltpu.SemaphoreType.DMA((4 * pairs,)),
        ],
        scalar=scalar,
        where=pl.ANY,
    )


def rebuild(pairs, second, rest):
    def kernel(second_in, rest_in, out, finest):
        for tile in range(2 * pairs):
            put_pairs(finest, (tile,), second_in[tile], rest_in[tile, :QUARTER])
            put_pairs(out, (tile,), finest[tile], rest_in[tile, QUARTER:])

    return call(
        kernel,
        [second, rest],
        [struct(2 * pairs, BLOCK, LANES)],
        scratch=[pltpu.VMEM((2 * pairs, HALF, LANES), F32)],
    )[0]


def take_apart(pairs, block_grad):
    def kernel(block, second, rest, finest):
        for tile in range(2 * pairs):
            finest[tile] = 2.0 * mean_rows(block, (tile,), 0, HALF, 2)
            rest[tile, QUARTER:] = 2.0 * half_difference(block, (tile,), 0, HALF)
            second[tile] = 2.0 * mean_rows(finest, (tile,), 0, QUARTER, 2)
            rest[tile, :QUARTER] = 2.0 * half_difference(finest, (tile,), 0, QUARTER)

    return call(
        kernel,
        [block_grad],
        [
            struct(2 * pairs, QUARTER, LANES),
            struct(2 * pairs, QUARTER + HALF, LANES),
        ],
        scratch=[pltpu.VMEM((2 * pairs, HALF, LANES), F32)],
    )


class Levels:
    def __init__(self, bits):
        self.bits = bits
        self.rows = BLOCK >> bits
        self.differences = [
            [(m, BLOCK >> m) for m in range(bits, step, -1)] for step in range(bits)
        ]
        whole = [0] + [BLOCK >> step for step in range(1, bits)]
        self.whole = Tree(1, whole)
        self.rough = Tree(1, [0] + [self.rows] * (bits - 1))
        self.fine = Tree(1, [0] + [rows - self.rows for rows in whole[1:]])
        self.pieces = []
        for level in range(1, bits):
            trees = (self.whole, self.rough, self.fine)
            for parts in zip(*(tree.held[level] for tree in trees)):
                self.pieces.append((level, parts[0][0], *(part[1] for part in parts)))

    def scratch(self):
        shapes = [(BLOCK >> m, LANES) for m in range(1, self.bits + 1)]
        return [pltpu.VMEM(shape, F32) for shape in shapes]

    def group_pieces(self):
        pieces = []
        for index, (level, step, whole, rough, _) in enumerate(self.pieces):
            factor = 1 << self.bits - level
            place = (2 + index) * self.rows
            pieces.append((step, whole, rough, BLOCK >> level, factor, place))
        return pieces


def coarsen_pair(lo, pairs, mine, received):
    def kernel(own, got, *outs):
        for tile in range(2 * pairs):
            outs[0][tile, : BLOCK // 4] = own[tile]
            outs[0][tile, BLOCK // 4 :] = got[tile]
            for index in range(1, lo.bits):
                outs[index][tile] = mean_rows(
                    outs[index - 1], (tile,), 0, BLOCK >> index + 1, 2
                )

    outs = [struct(2 * pairs, BLOCK >> step, LANES) for step in range(1, lo.bits + 1)]
    return call(kernel, [mine, received], outs)


def group_pieces(lo):
    own = BLOCK >> lo.bits
    factor = 1 << lo.bits
    pieces = [
        (-2, 0, BLOCK // 2, factor, own),
        (-1, 0, BLOCK // 2, factor, own + own // 2),
    ]
    filled = 2 * own
    for level in range(1, lo.bits):
        factor = 1 << lo.bits - level
        for step, row, rows in lo.held[level]:
            pieces.append((step, row, rows, factor, filled))
            filled += rows // factor
    return pieces


def coarsen_group(lo, hi, pairs, own, halves, arrived):
    pieces = group_pieces(lo)

    def kernel(own_in, *refs):
        ins = refs[: 2 + lo.bits]
        outs = refs[2 + lo.bits :]
        for tile in range(2 * pairs):
            outs[0][tile, pl.ds(0, BLOCK >> lo.bits)] = own_in[tile]
            for step, row, rows, factor, place in pieces:
                count = rows // factor
                outs[0][tile, pl.ds(place, count)] = mean_rows(
                    ins[2 + step], (tile,), row, count, factor
                )
            for step in range(1, hi.bits):
                outs[step][tile] = mean_rows(
                    outs[step - 1], (tile,), 0, BLOCK >> step, 2
                )

    outs = [struct(2 * pairs, BLOCK >> step, LANES) for step in range(hi.bits)]
    return call(kernel, [own, *halves, *arrived], outs)


def turn(pairs, mine, received):
    def kernel(own, got, turned):
        for tile in range(2 * pairs):
            both = jnp.concatenate([own[tile], got[tile]], axis=0).T
            turned[tile] = both * (SCALE * LOG2_E) if tile < pairs else both

    return call(kernel, [mine, received], [struct(2 * pairs, LANES, 2 * BLOCK)])[0]


def take_levels(levels, pairs, grads):
    trees = (levels.rough, levels.fine)

    def kernel(*refs):
        ins = refs[: levels.bits]
        rough = refs[levels.bits : 2 * levels.bits]
        fine = refs[2 * levels.bits : 3 * levels.bits]
        ladder = refs[3 * levels.bits :]
        for tile in range(2 * pairs):
            for level, step, row, rough_row, fine_row in levels.pieces:
                source = ladder[level - 1]
                source[...] = ins[step][tile, pl.ds(row, BLOCK >> level)]
                fine_row += sum(rows for _, rows in levels.differences[level])
                for m, rows in reversed(levels.differences[level]):
                    fine_row -= rows
                    part = 2.0 * half_difference(source, (), 0, rows)
                    fine[step][tile, pl.ds(fine_row, rows)] = part
                    ladder[m - 1][...] = 2.0 * mean_rows(source, (), 0, rows, 2)
                    source = ladder[m - 1]
                rough[step][tile, pl.ds(rough_row, levels.rows)] = source[...]

    outs = [
        struct(2 * pairs, tree.rows(step), LANES)
        for tree in trees
        for step in range(levels.bits)
    ]
    outs = call(kernel, grads, outs, scratch=levels.scratch())
    return outs[: levels.bits], outs[levels.bits :]


def spread_group(levels, hi, pairs, group_grads, grads):
    own_rows = levels.rows

    def kernel(*refs):
        steps = refs[: hi.bits]
        ins = refs[hi.bits : hi.bits + levels.bits]
        own_out, *outs = refs[hi.bits + levels.bits : -1]
        total = refs[-1]
        for tile in range(2 * pairs):
            total[tile] = steps[0][tile, pl.ds(0, BLOCK)]
            for step in range(1, hi.bits):
                above = steps[step][tile, pl.ds(0, BLOCK >> step)]
                add_spread(total, (tile,), 0, above, 1 << step)
            own_out[tile] = total[tile, pl.ds(0, own_rows)]
            for step, _, row, _, _, place in levels.group_pieces():
                rows = pl.ds(row, own_rows)
                part = total[tile, pl.ds(place, own_rows)]
                outs[step][tile, rows] = ins[step][tile, rows] + part
            outs[0][tile, pl.ds(ins[0].shape[1], own_rows)] = total[
                tile, pl.ds(own_rows, own_rows)
            ]

    shapes = [list(a.shape) for a in grads]
    shapes[0][1] += own_rows
    outs = [struct(2 * pairs, own_rows, LANES)] + [struct(*shape) for shape in shapes]
    own, *grads = call(
        kernel,
        [*group_grads, *grads],
        outs,
        scratch=[pltpu.VMEM((2 * pairs, BLOCK, LANES), F32)],
    )
    return own, grads


def spread_pair(levels, pairs, own_grad, rough, fine, block_second):
    own_rows = levels.rows

    def kernel(own, block, *refs):
        rough_in = refs[: levels.bits]
        fine_in = refs[levels.bits : 2 * levels.bits]
        mine, theirs, *ladder = refs[2 * levels.bits :]
        last = pl.ds(rough_in[0].shape[1] - own_rows, own_rows)
        for tile in range(2 * pairs):
            above = own[tile] + rough_in[0][tile, last]
            for step in range(1, levels.bits):
                above = above + rough_in[step][tile, pl.ds(0, own_rows)]
            filled = 0
            for m, rows in levels.differences[1]:
                part = fine_in[1][tile, pl.ds(filled, rows)]
                for step in range(2, min(m, levels.bits)):
                    part = part + fine_in[step][tile, pl.ds(filled, rows)]
                filled += rows
                put_pairs(ladder[m - 2], (), 0.5 * above, 0.5 * part)
                above = ladder[m - 2][...]
            mine[tile] = above[:QUARTER]
            theirs[tile] = above[QUARTER:] + block[tile]

    return call(
        kernel,
        [own_grad, block_second, *rough, *fine],
        [struct(2 * pairs, QUARTER, LANES)] * 2,
        scratch=levels.scratch(),
    )


def unpack(pairs, kept, arrived, features, scalar):
    def kernel(bit, *refs):
        outs = refs[4:]
        for which in range(2):
            for pair in range(pairs):
                for side, ref in ((bit[0], refs[which]), (1 - bit[0], refs[2 + which])):
                    column = side * (features // 2) + pair * LANES
                    column = pl.ds(pl.multiple_of(column, LANES), LANES)
                    outs[which][:, column] = ref[pair]

    return call(kernel, [*kept, *arrived], [struct(BLOCK, features)] * 2, scalar=scalar)


def finish(pairs, kept, rest, finest, seconds, features, scalar):
    def kernel(bit, kept_in, rest_in, f_mine, f_theirs, s_mine, s_theirs, *refs):
        outs, total, middle = refs[:2], refs[2], refs[3]
        for tile in range(2 * pairs):
            out = outs[tile // pairs]
            column = tile % pairs * LANES
            at = (tile,)
            total[tile] = kept_in[tile]
            add_spread(total, at, 0, f_mine[tile], 2)
            add_spread(total, at, 0, s_mine[tile], 4)
            place = bit[0] * (features // 2) + column
            out[:, pl.ds(pl.multiple_of(place, LANES), LANES)] = total[tile]
            put_pairs(middle, at, 0.5 * s_theirs[tile], 0.5 * rest_in[tile, :QUARTER])
            first = 0.5 * (middle[tile] + f_theirs[tile])
            put_pairs(total, at, first, 0.5 * rest_in[tile, QUARTER:])
            place = (1 - bit[0]) * (features // 2) + column
            out[:, pl.ds(pl.multiple_of(place, LANES), LANES)] = total[tile]

    return call(
        kernel,
        [kept, rest, *finest, *seconds],
        [struct(BLOCK, features)] * 2,
        scratch=[
            pltpu.VMEM((2 * pairs, BLOCK, LANES), F32),
            pltpu.VMEM((2 * pairs, HALF, LANES), F32),
        ],
        scalar=scalar,
    )


def on_device(queries, keys, values, cotangent):
    features = queries.shape[1]
    assert queries.shape[0] == BLOCK
    pairs = features // LANES // 2
    lo_bits = lax.axis_size("seqlo").bit_length() - 1
    levels = Levels(lo_bits - 1)
    lo = levels.whole
    hi_bits = lax.axis_size("seqhi").bit_length() - 1
    hi = Tree(lo_bits, [BLOCK >> step for step in range(hi_bits)])
    scalar = (lax.axis_index("seqlo") % 2).astype(jnp.int32).reshape(1)
    queries, keys, values, cotangent = [
        pltpu.with_memory_space_constraint(array, pltpu.HBM)
        for array in (queries, keys, values, cotangent)
    ]
    mine_kv, f_theirs, f_mine, c_send, c_mine, rest = pack_coarse(
        pairs, keys, values, scalar
    )
    second = exchange(c_send, 1)
    finest_theirs = exchange(f_theirs, 2)
    coarse = coarsen_pair(lo, pairs, c_mine, second)
    finest = exchange(ordered(f_mine, finest_theirs), 2)
    rest = exchange(ordered(rest, coarse[0]), 1)
    half = exchange(ordered(finest_theirs, rest), 1)
    kv = rebuild(pairs, second, rest)
    send_qg, mine_qg = pack(pairs, queries, cotangent, scalar)
    qg = exchange(ordered(send_qg, half), 1)
    zs = lo.gather([None, *coarse], (finest, send_qg))
    group = coarsen_group(
        lo, hi, pairs, ordered(coarse[-1], rest), [finest, half], zs
    )
    turned = turn(pairs, mine_qg, qg)
    rs = hi.gather(group, turned)
    block_sets = [(0, 0, 0, BLOCK), (0, 1, 0, BLOCK)]
    lo_sets = [(1, 2, 0, BLOCK // 2), (1, 3, 0, BLOCK // 2)]
    for level in range(lo.bits):
        for step, row, rows in lo.held[level]:
            lo_sets.append((1 + level, 4 + step, row, rows))
    hi_sets = []
    for level in range(hi.bits):
        for step, row, rows in hi.held[level]:
            hi_sets.append((lo_bits + level, step, row, rows))
    first_in = [mine_kv, kv, finest, half, *zs]
    *kept, tops, sums, partial = attend_first(
        pairs, block_sets + lo_sets, first_in, turned
    )
    *rs_grads, o_keep, o_send, g_scaled, row_dot, dq = attend_last(
        pairs, hi_sets, rs, turned, tops, sums, partial
    )
    shapes = [(2 * pairs, *a.shape[1:]) for a in first_in]
    finest_grad, half_grad, *zs_grads, dq = attend_back(
        pairs,
        [(level, index - 2, row, rows) for level, index, row, rows in lo_sets],
        shapes[2:],
        BOTH,
        kept,
        turned,
        g_scaled,
        row_dot,
        dq,
        False,
    )
    kv_keep, kv_send, dq_keep, dq_send = attend_back(
        pairs, block_sets, shapes[:2], 0, kept, turned, g_scaled, row_dot, dq, True
    )
    rough_grads, fine_grads = take_levels(levels, pairs, zs_grads)
    group_grads = hi.scatter(rs_grads)
    half_back = exchange(ordered(half_grad, group_grads[0]), 1)
    o_back = exchange(o_send, 1)
    fine_back, finest_mine = levels.fine.scatter(fine_grads, finest_grad)
    block_second, rest_grad = take_apart(pairs, kv_send)
    split_at = rest_grad.shape[1]
    bulk = jnp.concatenate([rest_grad, dq_send.reshape(2 * pairs, HALF, LANES)], axis=1)
    bulk = exchange(ordered(bulk, o_back), 1)
    rest_back = bulk[:, :split_at]
    dq_back = bulk[:, split_at:].reshape(pairs, BLOCK, LANES)
    group_grads[-1] = ordered(group_grads[-1], kv_send)
    own_grad, rough_grads = spread_group(levels, hi, pairs, group_grads, rough_grads)
    rough_back = levels.rough.scatter(rough_grads)
    finest_theirs = exchange(ordered(half_back, rough_back[0]), 2)
    own_grad = ordered(own_grad, (rest_back, dq_back))
    second_mine, second_send = spread_pair(
        levels, pairs, own_grad, rough_back, fine_back, block_second
    )
    second_theirs = exchange(second_send, 1)
    attended, query_grad = unpack(
        pairs, (o_keep, dq_keep), (o_back, dq_back), features, scalar
    )
    key_grad, value_grad = finish(
        pairs,
        kv_keep,
        rest_back,
        (finest_mine, finest_theirs),
        (second_mine, second_theirs),
        features,
        scalar,
    )
    return attended, query_grad, key_grad, value_grad


def solution(mesh):
    spec = P(AXES, None)
    return jax.shard_map(
        on_device,
        mesh=mesh,
        in_specs=(spec,) * 4,
        out_specs=(spec,) * 4,
        check_vma=False,
    )
```

profile of v0, /device:TPU:0, one launch (start us, length us, event | category | flops | bytes accessed | tf_op | source)
XLA Modules:
  0.0 68.5 jit_solution(2597868050363758648)
XLA Ops:
  0.6 1.3 %shard_map.91 = (f32[6,128,128]{2,1,0:T(8,128)S(1)}, f32[6,64,128]{2,1,0:T(8,128)S(1)}, f32[6,64,128]{2,1,0:T(8,128)S(1)}, f32[6,32,128]{2,1,0:T(8,128)S(1)}, f3...) custom-call(s32[1]{0:T(128)} %bitcast.bit, f32[128,768]{1,0:T(8,128)} %k.1, f32[128,768]{1,0:T(8,128)} %v.1), custom_call_target="tpu_custom_call" | custom-call | bytes 2064388 | tf_op jit(solution)/shard_map/pallas_call | solution.py:34
  1.9 3.0 %collective-permute-start.1 = (f32[6,32,128]{2,1,0:T(8,128)S(1)}, f32[6,32,128]{2,1,0:T(8,128)S(1)}, u32[]{:S(2)}, u32[]{:S(2)}) collective-permute-start(f32[6,32,128]{2,1,0:T(8,128)S(1)} %get-tuple-element.130), channel_id=1, source_target_pairs={{0,1},{1,0},{2,3},{3,2},{4,5},{5,4},{6,7},{7,6},{8,9},{9,8},{10,11... | collective-permute-start | bytes 294920 | tf_op jit(solution)/shard_map/ppermute | solution.py:49
  5.0 1.6 %collective-permute-start = (f32[6,64,128]{2,1,0:T(8,128)S(1)}, f32[6,64,128]{2,1,0:T(8,128)S(1)}, u32[]{:S(2)}, u32[]{:S(2)}) collective-permute-start(f32[6,64,128]{2,1,0:T(8,128)S(1)} %get-tuple-element.127), channel_id=1, source_target_pairs={{0,2},{1,3},{2,0},{3,1},{4,6},{5,7},{6,4},{7,5},{8,10},{9,11},{10,... | collective-permute-start | bytes 589832 | tf_op jit(solution)/shard_map/ppermute | solution.py:49
  6.5 1.2 %collective-permute-done.1.got.second_in = f32[6,32,128]{2,1,0:T(8,128)S(1)} collective-permute-done((f32[6,32,128]{2,1,0:T(8,128)S(1)}, f32[6,32,128]{2,1,0:T(8,128)S(1)}, u32[]{:S(2)}, u32[]{:S(2)}) %collective-permute-start.1) | collective-permute-done | bytes 98336 | tf_op jit(solution)/shard_map/ppermute | solution.py:49
  7.8 1.9 %collective-permute-start.2 = (f32[6,96,128]{2,1,0:T(8,128)S(1)}, f32[6,96,128]{2,1,0:T(8,128)S(1)}, u32[]{:S(2)}, u32[]{:S(2)}) collective-permute-start(f32[6,96,128]{2,1,0:T(8,128)S(1)} %get-tuple-element.132), channel_id=1, source_target_pairs={{0,1},{1,0},{2,3},{3,2},{4,5},{5,4},{6,7},{7,6},{8,9},{9,8},{10,11... | collective-permute-start | bytes 884744 | tf_op jit(solution)/shard_map/ppermute | solution.py:49
  9.7 2.6 %collective-permute-start.6 = (f32[6,64,128]{2,1,0:T(8,128)S(1)}, f32[6,64,128]{2,1,0:T(8,128)S(1)}, u32[]{:S(2)}, u32[]{:S(2)}) collective-permute-start(f32[6,64,128]{2,1,0:T(8,128)S(1)} %get-tuple-element.131), channel_id=1, source_target_pairs={{0,4},{1,5},{2,6},{3,7},{4,0},{5,1},{6,2},{7,3},{8,12},{9,13},{10,... | collective-permute-start | bytes 589832 | tf_op jit(solution)/shard_map/ppermute | solution.py:49
  12.3 1.6 %collective-permute-start.5 = (f32[6,64,128]{2,1,0:T(8,128)S(1)}, f32[6,64,128]{2,1,0:T(8,128)S(1)}, u32[]{:S(2)}, u32[]{:S(2)}) collective-permute-start(f32[6,64,128]{2,1,0:T(8,128)S(1)} %get-tuple-element.137), channel_id=1, source_target_pairs={{0,2},{1,3},{2,0},{3,1},{4,6},{5,7},{6,4},{7,5},{8,10},{9,11},{10,... | collective-permute-start | bytes 589832 | tf_op jit(solution)/shard_map/ppermute | solution.py:49
  13.9 2.2 %collective-permute-done.2.rest_in = f32[6,96,128]{2,1,0:T(8,128)S(1)} collective-permute-done((f32[6,96,128]{2,1,0:T(8,128)S(1)}, f32[6,96,128]{2,1,0:T(8,128)S(1)}, u32[]{:S(2)}, u32[]{:S(2)}) %collective-permute-start.2) | collective-permute-done | bytes 294944 | tf_op jit(solution)/shard_map/ppermute | solution.py:49
  16.1 1.2 %collective-permute-start.3 = (f32[6,64,128]{2,1,0:T(8,128)S(1)}, f32[6,64,128]{2,1,0:T(8,128)S(1)}, u32[]{:S(2)}, u32[]{:S(2)}) collective-permute-start(f32[6,64,128]{2,1,0:T(8,128)S(1)} %collective-permute-done), channel_id=1, source_target_pairs={{0,1},{1,0},{2,3},{3,2},{4,5},{5,4},{6,7},{7,6},{8,9},{9,8},{10,11... | collective-permute-start | bytes 589832 | tf_op jit(solution)/shard_map/ppermute | solution.py:49
  17.3 1.3 %shard_map.90 = (f32[6,128,128]{2,1,0:T(8,128)S(1)}, f32[6,128,128]{2,1,0:T(8,128)S(1)}) custom-call(s32[1]{0:T(128)} %bitcast.bit, f32[128,768]{1,0:T(8,128)} %one.1, f32[128,768]{1,0:T(8,128)} %two.1), custom_call_target="tpu_custom_call" | custom-call | bytes 1572868 | tf_op jit(solution)/shard_map/pallas_call | solution.py:34
  18.6 1.6 %collective-permute-done.6.refs_5_.refs_3_ = f32[6,64,128]{2,1,0:T(8,128)S(1)} collective-permute-done((f32[6,64,128]{2,1,0:T(8,128)S(1)}, f32[6,64,128]{2,1,0:T(8,128)S(1)}, u32[]{:S(2)}, u32[]{:S(2)}) %collective-permute-start.6) | collective-permute-done | bytes 196640 | tf_op jit(solution)/shard_map/ppermute | solution.py:49
  20.3 1.5 %collective-permute-start.7 = (f32[6,64,128]{2,1,0:T(8,128)S(1)}, f32[6,64,128]{2,1,0:T(8,128)S(1)}, u32[]{:S(2)}, u32[]{:S(2)}) collective-permute-start(f32[6,64,128]{2,1,0:T(8,128)S(1)} %collective-permute-done.6.refs_5_.refs_3_), channel_id=1, source_target_pairs={{0,2},{1,3},{2,0},{3,1},{4,6},{5,7},{6,4},{7,5},{8,10},{9,11},{10,... | collective-permute-start | bytes 589832 | tf_op jit(solution)/shard_map/ppermute | solution.py:49
  21.8 1.2 %collective-permute-start.4 = (f32[6,128,128]{2,1,0:T(8,128)S(1)}, f32[6,128,128]{2,1,0:T(8,128)S(1)}, u32[]{:S(2)}, u32[]{:S(2)}) collective-permute-start(f32[6,128,128]{2,1,0:T(8,128)S(1)} %get-tuple-element.134), channel_id=1, source_target_pairs={{0,1},{1,0},{2,3},{3,2},{4,5},{5,4},{6,7},{7,6},{8,9},{9,8},{10,11... | collective-permute-start | bytes 1179656 | tf_op jit(solution)/shard_map/ppermute | solution.py:49
  23.0 3.0 %collective-permute-done.7.refs_4_.refs_2_ = f32[6,64,128]{2,1,0:T(8,128)S(1)} collective-permute-done((f32[6,64,128]{2,1,0:T(8,128)S(1)}, f32[6,64,128]{2,1,0:T(8,128)S(1)}, u32[]{:S(2)}, u32[]{:S(2)}) %collective-permute-start.7) | collective-permute-done | bytes 196640 | tf_op jit(solution)/shard_map/ppermute | solution.py:49
  26.1 1.6 %collective-permute-start.8 = (f32[6,64,128]{2,1,0:T(8,128)S(1)}, f32[6,64,128]{2,1,0:T(8,128)S(1)}, u32[]{:S(2)}, u32[]{:S(2)}) collective-permute-start(f32[6,64,128]{2,1,0:T(8,128)S(1)} %get-tuple-element.145), channel_id=1, source_target_pairs={{0,16},{1,17},{2,18},{3,19},{4,20},{5,21},{6,22},{7,23},{8,24},{9,... | collective-permute-start | bytes 589832 | tf_op jit(solution)/shard_map/ppermute | solution.py:49
  27.6 4.2 %collective-permute-done.8.refs_1_ = f32[6,64,128]{2,1,0:T(8,128)S(1)} collective-permute-done((f32[6,64,128]{2,1,0:T(8,128)S(1)}, f32[6,64,128]{2,1,0:T(8,128)S(1)}, u32[]{:S(2)}, u32[]{:S(2)}) %collective-permute-start.8) | collective-permute-done | bytes 196640 | tf_op jit(solution)/shard_map/ppermute | solution.py:49
  32.3 2.4 %shard_map.95 = (bf16[6,128,512]{2,1,0:T(8,128)(2,1)S(1)}, bf16[6,512,128]{2,1,0:T(8,128)(2,1)S(1)}, bf16[6,2,512,256]{3,2,1,0:T(8,128)(2,1)S(1)}, f32[6,1,256]{...) custom-call(f32[6,128,256]{2,1,0:T(8,128)S(1)} %shard_map.93.turn_in, ...), custom_call_target="tpu_custom_call" | custom-call | flops 805306368 | bytes 12201984 | tf_op jit(solution)/shard_map/pallas_call | solution.py:34
  34.6 2.5 %shard_map.97 = (f32[6,192,128]{2,1,0:T(8,128)S(1)}, f32[6,64,128]{2,1,0:T(8,128)S(1)}, f32[3,128,128]{2,1,0:T(8,128)S(1)}, f32[3,128,128]{2,1,0:T(8,128)S(1)}, ...) custom-call(f32[6,128,256]{2,1,0:T(8,128)S(1)} %shard_map.93.turn_in, ...), custom_call_target="tpu_custom_call" | custom-call | flops 1207959552 | bytes 3950592 | tf_op jit(solution)/shard_map/pallas_call | solution.py:34
  38.6 1.5 %shard_map.98 = (f32[6,64,128]{2,1,0:T(8,128)S(1)}, f32[6,64,128]{2,1,0:T(8,128)S(1)}, f32[6,64,128]{2,1,0:T(8,128)S(1)}, f32[6,64,128]{2,1,0:T(8,128)S(1)}, f32[6,64,256]{2,1,0:T(8,128)S(1)}) custom-call(f32[6,128,256]{2,1,0:T(8,128)S(1)} %shard_map.93.turn_in, bf16[6,128,512]{2,1,0:T(8,128)(2,1)S(1)} %get-tuple-element.148.kt, ...), custom_call_target="tpu_custom_call" | custom-call | flops 805306368 | bytes 12195840 | tf_op jit(solution)/shard_map/pallas_call | solution.py:34
  40.2 1.2 %collective-permute-start.12 = (f32[6,96,128]{2,1,0:T(8,128)S(1)}, f32[6,96,128]{2,1,0:T(8,128)S(1)}, u32[]{:S(2)}, u32[]{:S(2)}) collective-permute-start(f32[6,96,128]{2,1,0:T(8,128)S(1)} %pad_maximum_fusion.2), channel_id=1, source_target_pairs={{0,2},{1,3},{2,0},{3,1},{4,6},{5,7},{6,4},{7,5},{8,10},{9,11},{10,... | collective-permute-start | bytes 884744 | tf_op jit(solution)/shard_map/ppermute | solution.py:49
  41.5 1.6 %collective-permute-start.15 = (f32[6,64,128]{2,1,0:T(8,128)S(1)}, f32[6,64,128]{2,1,0:T(8,128)S(1)}, u32[]{:S(2)}, u32[]{:S(2)}) collective-permute-start(f32[6,64,128]{2,1,0:T(8,128)S(1)} %slice_add_fusion), channel_id=1, source_target_pairs={{0,16},{1,17},{2,18},{3,19},{4,20},{5,21},{6,22},{7,23},{8,24},{9,... | collective-permute-start | bytes 589832 | tf_op jit(solution)/shard_map/ppermute | solution.py:49
  43.0 1.6 %shard_map.99 = (f32[6,128,128]{2,1,0:T(8,128)S(1)}, f32[6,128,128]{2,1,0:T(8,128)S(1)}, f32[3,128,128]{2,1,0:T(8,128)S(1)}, f32[3,128,128]{2,1,0:T(8,128)S(1)}) custom-call(f32[6,128,256]{2,1,0:T(8,128)S(1)} %shard_map.93.turn_in, bf16[6,128,512]{2,1,0:T(8,128)(2,1)S(1)} %get-tuple-element.148.kt, bf16[6,512,128]{2,1,0:T(8,128)(2,1)S(1)} %get-tuple-element.149.vc, ...), custom_call_target="tpu_custom_call" | custom-call | flops 805306368 | bytes 12195840 | tf_op jit(solution)/shard_map/pallas_call | solution.py:34
  44.8 1.6 %collective-permute-start.11 = (f32[6,160,128]{2,1,0:T(8,128)S(1)}, f32[6,160,128]{2,1,0:T(8,128)S(1)}, u32[]{:S(2)}, u32[]{:S(2)}) collective-permute-start(f32[6,160,128]{2,1,0:T(8,128)S(1)} %pad_maximum_fusion.1), channel_id=1, source_target_pairs={{0,1},{1,0},{2,3},{3,2},{4,5},{5,4},{6,7},{7,6},{8,9},{9,8},{10,11... | collective-permute-start | bytes 1474568 | tf_op jit(solution)/shard_map/ppermute | solution.py:49
  46.4 1.5 %collective-permute-done.15.refs_1_ = f32[6,64,128]{2,1,0:T(8,128)S(1)} collective-permute-done((f32[6,64,128]{2,1,0:T(8,128)S(1)}, f32[6,64,128]{2,1,0:T(8,128)S(1)}, u32[]{:S(2)}, u32[]{:S(2)}) %collective-permute-start.15) | collective-permute-done | bytes 196640 | tf_op jit(solution)/shard_map/ppermute | solution.py:49
  49.0 2.8 %collective-permute-start.19 = (f32[6,32,128]{2,1,0:T(8,128)S(1)}, f32[6,32,128]{2,1,0:T(8,128)S(1)}, u32[]{:S(2)}, u32[]{:S(2)}) collective-permute-start(f32[6,32,128]{2,1,0:T(8,128)S(1)} %get-tuple-element.186), channel_id=1, source_target_pairs={{0,4},{1,5},{2,6},{3,7},{4,0},{5,1},{6,2},{7,3},{8,12},{9,13},{10,... | collective-permute-start | bytes 294920 | tf_op jit(solution)/shard_map/ppermute | solution.py:49
  51.8 1.5 %collective-permute-start.14 = (f32[6,64,128]{2,1,0:T(8,128)S(1)}, f32[6,64,128]{2,1,0:T(8,128)S(1)}, u32[]{:S(2)}, u32[]{:S(2)}) collective-permute-start(f32[6,64,128]{2,1,0:T(8,128)S(1)} %get-tuple-element.170), channel_id=1, source_target_pairs={{0,1},{1,0},{2,3},{3,2},{4,5},{5,4},{6,7},{7,6},{8,9},{9,8},{10,11... | collective-permute-start | bytes 589832 | tf_op jit(solution)/shard_map/ppermute | solution.py:49
  53.4 2.7 %collective-permute-done.16.refs_0_ = f32[6,64,128]{2,1,0:T(8,128)S(1)} collective-permute-done((f32[6,64,128]{2,1,0:T(8,128)S(1)}, f32[6,64,128]{2,1,0:T(8,128)S(1)}, u32[]{:S(2)}, u32[]{:S(2)}) %collective-permute-start.16) | collective-permute-done | bytes 196640 | tf_op jit(solution)/shard_map/ppermute | solution.py:49
  56.1 2.6 %collective-permute-start.18 = (f32[6,32,128]{2,1,0:T(8,128)S(1)}, f32[6,32,128]{2,1,0:T(8,128)S(1)}, u32[]{:S(2)}, u32[]{:S(2)}) collective-permute-start(f32[6,32,128]{2,1,0:T(8,128)S(1)} %slice_add_fusion.1), channel_id=1, source_target_pairs={{0,4},{1,5},{2,6},{3,7},{4,0},{5,1},{6,2},{7,3},{8,12},{9,13},{10,... | collective-permute-start | bytes 294920 | tf_op jit(solution)/shard_map/ppermute | solution.py:49
  58.7 2.7 %collective-permute-done.14 = f32[6,64,128]{2,1,0:T(8,128)S(1)} collective-permute-done((f32[6,64,128]{2,1,0:T(8,128)S(1)}, f32[6,64,128]{2,1,0:T(8,128)S(1)}, u32[]{:S(2)}, u32[]{:S(2)}) %collective-permute-start.14) | collective-permute-done | bytes 196640 | tf_op jit(solution)/shard_map/ppermute | solution.py:49
  61.4 1.3 %collective-permute-start.17 = (f32[6,64,128]{2,1,0:T(8,128)S(1)}, f32[6,64,128]{2,1,0:T(8,128)S(1)}, u32[]{:S(2)}, u32[]{:S(2)}) collective-permute-start(f32[6,64,128]{2,1,0:T(8,128)S(1)} %collective-permute-done.14), channel_id=1, source_target_pairs={{0,2},{1,3},{2,0},{3,1},{4,6},{5,7},{6,4},{7,5},{8,10},{9,11},{10,... | collective-permute-start | bytes 589832 | tf_op jit(solution)/shard_map/ppermute | solution.py:49
  64.7 2.4 %collective-permute-done.17.f_theirs = f32[6,64,128]{2,1,0:T(8,128)S(1)} collective-permute-done((f32[6,64,128]{2,1,0:T(8,128)S(1)}, f32[6,64,128]{2,1,0:T(8,128)S(1)}, u32[]{:S(2)}, u32[]{:S(2)}) %collective-permute-start.17) | collective-permute-done | bytes 196640 | tf_op jit(solution)/shard_map/ppermute | solution.py:49
  67.5 1.0 %shard_map.105 = (f32[128,768]{1,0:T(8,128)}, f32[128,768]{1,0:T(8,128)}) custom-call(s32[1]{0:T(128)} %bitcast.bit, f32[6,128,128]{2,1,0:T(8,128)S(1)} %get-tuple-element.163.kept_in, f32[6,96,128]{2,1,0:T(8,128)S(1)} %slice.82.rest_in, f32[6,64,128]{2,1,0:T(8,128)S(1)} %slice.83.f_mine, f32[6,64,128]{2,1,0:T(8,128)S(1)} %collective-permute-done.17.f_theirs, ...), custom_call_target="tpu_custom_call" | custom-call | bytes 2064388 | tf_op jit(solution)/shard_map/pallas_call | solution.py:34
  (35 shorter events, 5.9 us)
Async XLA Ops:
  1.9 5.8 %collective-permute-start.1 = (f32[6,32,128]{2,1,0:T(8,128)S(1)}, f32[6,32,128]{2,1,0:T(8,128)S(1)}, u32[]{:S(2)}, u32[]{:S(2)}) collective-permute-start(f32[6,32,128]{2,1,0:T(8,128)S(1)} %get-tuple-element.130), channel_id=1, source_target_pairs={{0,1},{1,0},{2,3},{3,2},{4,5},{5,4},{6,7},{7,6},{8,9},{9,8},{10,11... | collective-permute-start | bytes 294920 | tf_op jit(solution)/shard_map/ppermute | solution.py:49
  5.0 7.3 %collective-permute-start = (f32[6,64,128]{2,1,0:T(8,128)S(1)}, f32[6,64,128]{2,1,0:T(8,128)S(1)}, u32[]{:S(2)}, u32[]{:S(2)}) collective-permute-start(f32[6,64,128]{2,1,0:T(8,128)S(1)} %get-tuple-element.127), channel_id=1, source_target_pairs={{0,2},{1,3},{2,0},{3,1},{4,6},{5,7},{6,4},{7,5},{8,10},{9,11},{10,... | collective-permute-start | bytes 589832 | tf_op jit(solution)/shard_map/ppermute | solution.py:49
  7.8 8.3 %collective-permute-start.2 = (f32[6,96,128]{2,1,0:T(8,128)S(1)}, f32[6,96,128]{2,1,0:T(8,128)S(1)}, u32[]{:S(2)}, u32[]{:S(2)}) collective-permute-start(f32[6,96,128]{2,1,0:T(8,128)S(1)} %get-tuple-element.132), channel_id=1, source_target_pairs={{0,1},{1,0},{2,3},{3,2},{4,5},{5,4},{6,7},{7,6},{8,9},{9,8},{10,11... | collective-permute-start | bytes 884744 | tf_op jit(solution)/shard_map/ppermute | solution.py:49
  9.7 10.4 %collective-permute-start.6 = (f32[6,64,128]{2,1,0:T(8,128)S(1)}, f32[6,64,128]{2,1,0:T(8,128)S(1)}, u32[]{:S(2)}, u32[]{:S(2)}) collective-permute-start(f32[6,64,128]{2,1,0:T(8,128)S(1)} %get-tuple-element.131), channel_id=1, source_target_pairs={{0,4},{1,5},{2,6},{3,7},{4,0},{5,1},{6,2},{7,3},{8,12},{9,13},{10,... | collective-permute-start | bytes 589832 | tf_op jit(solution)/shard_map/ppermute | solution.py:49
  12.3 8.0 %collective-permute-start.5 = (f32[6,64,128]{2,1,0:T(8,128)S(1)}, f32[6,64,128]{2,1,0:T(8,128)S(1)}, u32[]{:S(2)}, u32[]{:S(2)}) collective-permute-start(f32[6,64,128]{2,1,0:T(8,128)S(1)} %get-tuple-element.137), channel_id=1, source_target_pairs={{0,2},{1,3},{2,0},{3,1},{4,6},{5,7},{6,4},{7,5},{8,10},{9,11},{10,... | collective-permute-start | bytes 589832 | tf_op jit(solution)/shard_map/ppermute | solution.py:49
  16.1 5.7 %collective-permute-start.3 = (f32[6,64,128]{2,1,0:T(8,128)S(1)}, f32[6,64,128]{2,1,0:T(8,128)S(1)}, u32[]{:S(2)}, u32[]{:S(2)}) collective-permute-start(f32[6,64,128]{2,1,0:T(8,128)S(1)} %collective-permute-done), channel_id=1, source_target_pairs={{0,1},{1,0},{2,3},{3,2},{4,5},{5,4},{6,7},{7,6},{8,9},{9,8},{10,11... | collective-permute-start | bytes 589832 | tf_op jit(solution)/shard_map/ppermute | solution.py:49
  20.3 5.7 %collective-permute-start.7 = (f32[6,64,128]{2,1,0:T(8,128)S(1)}, f32[6,64,128]{2,1,0:T(8,128)S(1)}, u32[]{:S(2)}, u32[]{:S(2)}) collective-permute-start(f32[6,64,128]{2,1,0:T(8,128)S(1)} %collective-permute-done.6.refs_5_.refs_3_), channel_id=1, source_target_pairs={{0,2},{1,3},{2,0},{3,1},{4,6},{5,7},{6,4},{7,5},{8,10},{9,11},{10,... | collective-permute-start | bytes 589832 | tf_op jit(solution)/shard_map/ppermute | solution.py:49
  21.8 10.1 %collective-permute-start.4 = (f32[6,128,128]{2,1,0:T(8,128)S(1)}, f32[6,128,128]{2,1,0:T(8,128)S(1)}, u32[]{:S(2)}, u32[]{:S(2)}) collective-permute-start(f32[6,128,128]{2,1,0:T(8,128)S(1)} %get-tuple-element.134), channel_id=1, source_target_pairs={{0,1},{1,0},{2,3},{3,2},{4,5},{5,4},{6,7},{7,6},{8,9},{9,8},{10,11... | collective-permute-start | bytes 1179656 | tf_op jit(solution)/shard_map/ppermute | solution.py:49
  26.1 5.7 %collective-permute-start.8 = (f32[6,64,128]{2,1,0:T(8,128)S(1)}, f32[6,64,128]{2,1,0:T(8,128)S(1)}, u32[]{:S(2)}, u32[]{:S(2)}) collective-permute-start(f32[6,64,128]{2,1,0:T(8,128)S(1)} %get-tuple-element.145), channel_id=1, source_target_pairs={{0,16},{1,17},{2,18},{3,19},{4,20},{5,21},{6,22},{7,23},{8,24},{9,... | collective-permute-start | bytes 589832 | tf_op jit(solution)/shard_map/ppermute | solution.py:49
  32.1 2.5 %collective-permute-start.9 = (f32[6,192,128]{2,1,0:T(8,128)S(1)}, f32[6,192,128]{2,1,0:T(8,128)S(1)}, u32[]{:S(2)}, u32[]{:S(2)}) collective-permute-start(f32[6,192,128]{2,1,0:T(8,128)S(1)} %pad_maximum_fusion), channel_id=1, source_target_pairs={{0,8},{1,9},{2,10},{3,11},{4,12},{5,13},{6,14},{7,15},{8,0},{9,1},... | collective-permute-start | bytes 1769480 | tf_op jit(solution)/shard_map/ppermute | solution.py:49
  37.2 4.3 %collective-permute-start.13 = (f32[6,192,128]{2,1,0:T(8,128)S(1)}, f32[6,192,128]{2,1,0:T(8,128)S(1)}, u32[]{:S(2)}, u32[]{:S(2)}) collective-permute-start(f32[6,192,128]{2,1,0:T(8,128)S(1)} %get-tuple-element.169), channel_id=1, source_target_pairs={{0,8},{1,9},{2,10},{3,11},{4,12},{5,13},{6,14},{7,15},{8,0},{9,1},... | collective-permute-start | bytes 1769480 | tf_op jit(solution)/shard_map/ppermute | solution.py:49
  37.8 7.0 %collective-permute-start.10 = (f32[3,128,128]{2,1,0:T(8,128)S(1)}, f32[3,128,128]{2,1,0:T(8,128)S(1)}, u32[]{:S(2)}, u32[]{:S(2)}) collective-permute-start(f32[3,128,128]{2,1,0:T(8,128)S(1)} %get-tuple-element.156), channel_id=1, source_target_pairs={{0,1},{1,0},{2,3},{3,2},{4,5},{5,4},{6,7},{7,6},{8,9},{9,8},{10,11... | collective-permute-start | bytes 589832 | tf_op jit(solution)/shard_map/ppermute | solution.py:49
  40.2 8.8 %collective-permute-start.12 = (f32[6,96,128]{2,1,0:T(8,128)S(1)}, f32[6,96,128]{2,1,0:T(8,128)S(1)}, u32[]{:S(2)}, u32[]{:S(2)}) collective-permute-start(f32[6,96,128]{2,1,0:T(8,128)S(1)} %pad_maximum_fusion.2), channel_id=1, source_target_pairs={{0,2},{1,3},{2,0},{3,1},{4,6},{5,7},{6,4},{7,5},{8,10},{9,11},{10,... | collective-permute-start | bytes 884744 | tf_op jit(solution)/shard_map/ppermute | solution.py:49
  41.5 6.4 %collective-permute-start.15 = (f32[6,64,128]{2,1,0:T(8,128)S(1)}, f32[6,64,128]{2,1,0:T(8,128)S(1)}, u32[]{:S(2)}, u32[]{:S(2)}) collective-permute-start(f32[6,64,128]{2,1,0:T(8,128)S(1)} %slice_add_fusion), channel_id=1, source_target_pairs={{0,16},{1,17},{2,18},{3,19},{4,20},{5,21},{6,22},{7,23},{8,24},{9,... | collective-permute-start | bytes 589832 | tf_op jit(solution)/shard_map/ppermute | solution.py:49
  44.8 17.9 %collective-permute-start.11 = (f32[6,160,128]{2,1,0:T(8,128)S(1)}, f32[6,160,128]{2,1,0:T(8,128)S(1)}, u32[]{:S(2)}, u32[]{:S(2)}) collective-permute-start(f32[6,160,128]{2,1,0:T(8,128)S(1)} %pad_maximum_fusion.1), channel_id=1, source_target_pairs={{0,1},{1,0},{2,3},{3,2},{4,5},{5,4},{6,7},{7,6},{8,9},{9,8},{10,11... | collective-permute-start | bytes 1474568 | tf_op jit(solution)/shard_map/ppermute | solution.py:49
  48.0 8.1 %collective-permute-start.16 = (f32[6,64,128]{2,1,0:T(8,128)S(1)}, f32[6,64,128]{2,1,0:T(8,128)S(1)}, u32[]{:S(2)}, u32[]{:S(2)}) collective-permute-start(f32[6,64,128]{2,1,0:T(8,128)S(1)} %get-tuple-element.175), channel_id=1, source_target_pairs={{0,2},{1,3},{2,0},{3,1},{4,6},{5,7},{6,4},{7,5},{8,10},{9,11},{10,... | collective-permute-start | bytes 589832 | tf_op jit(solution)/shard_map/ppermute | solution.py:49
  49.0 13.7 %collective-permute-start.19 = (f32[6,32,128]{2,1,0:T(8,128)S(1)}, f32[6,32,128]{2,1,0:T(8,128)S(1)}, u32[]{:S(2)}, u32[]{:S(2)}) collective-permute-start(f32[6,32,128]{2,1,0:T(8,128)S(1)} %get-tuple-element.186), channel_id=1, source_target_pairs={{0,4},{1,5},{2,6},{3,7},{4,0},{5,1},{6,2},{7,3},{8,12},{9,13},{10,... | collective-permute-start | bytes 294920 | tf_op jit(solution)/shard_map/ppermute | solution.py:49
  51.8 9.6 %collective-permute-start.14 = (f32[6,64,128]{2,1,0:T(8,128)S(1)}, f32[6,64,128]{2,1,0:T(8,128)S(1)}, u32[]{:S(2)}, u32[]{:S(2)}) collective-permute-start(f32[6,64,128]{2,1,0:T(8,128)S(1)} %get-tuple-element.170), channel_id=1, source_target_pairs={{0,1},{1,0},{2,3},{3,2},{4,5},{5,4},{6,7},{7,6},{8,9},{9,8},{10,11... | collective-permute-start | bytes 589832 | tf_op jit(solution)/shard_map/ppermute | solution.py:49
  56.1 6.6 %collective-permute-start.18 = (f32[6,32,128]{2,1,0:T(8,128)S(1)}, f32[6,32,128]{2,1,0:T(8,128)S(1)}, u32[]{:S(2)}, u32[]{:S(2)}) collective-permute-start(f32[6,32,128]{2,1,0:T(8,128)S(1)} %slice_add_fusion.1), channel_id=1, source_target_pairs={{0,4},{1,5},{2,6},{3,7},{4,0},{5,1},{6,2},{7,3},{8,12},{9,13},{10,... | collective-permute-start | bytes 294920 | tf_op jit(solution)/shard_map/ppermute | solution.py:49
  61.4 5.7 %collective-permute-start.17 = (f32[6,64,128]{2,1,0:T(8,128)S(1)}, f32[6,64,128]{2,1,0:T(8,128)S(1)}, u32[]{:S(2)}, u32[]{:S(2)}) collective-permute-start(f32[6,64,128]{2,1,0:T(8,128)S(1)} %collective-permute-done.14), channel_id=1, source_target_pairs={{0,2},{1,3},{2,0},{3,1},{4,6},{5,7},{6,4},{7,5},{8,10},{9,11},{10,... | collective-permute-start | bytes 589832 | tf_op jit(solution)/shard_map/ppermute | solution.py:49
  62.8 4.7 %collective-permute-start.20 = (f32[6,32,128]{2,1,0:T(8,128)S(1)}, f32[6,32,128]{2,1,0:T(8,128)S(1)}, u32[]{:S(2)}, u32[]{:S(2)}) collective-permute-start(f32[6,32,128]{2,1,0:T(8,128)S(1)} %get-tuple-element.183), channel_id=1, source_target_pairs={{0,1},{1,0},{2,3},{3,2},{4,5},{5,4},{6,7},{7,6},{8,9},{9,8},{10,11... | collective-permute-start | bytes 294920 | tf_op jit(solution)/shard_map/ppermute | solution.py:49
where the time goes:
time: 68.7 us; the launch traced here: 68.5 us
  starting transfers between devices  31.9 us (46%)
  waiting for transfers between devices  22.2 us (32%)
  Pallas kernels  13.4 us (20%)
  between operations  0.82 us (1%)
    ppermute x21, starting transfers between devices, exchange(): return lax.ppermute(value, AXES, [(i, i ^ offset) for i in range(count)])  31.9 us
    ppermute x21, waiting for transfers between devices, exchange(): return lax.ppermute(value, AXES, [(i, i ^ offset) for i in range(count)])  22.2 us
    pallas_call x16, Pallas kernels, call(): pl.pallas_call(kernel, out_shape=list(outs), in_specs=in_specs, out_specs...  13.4 us
  transfers between devices with their start and end apart: 21, of which 12 were waited for; matrix products, arithmetic and copies ran while one was open for 0% of the time, Pallas kernels for 12%

commit v1 on v0

--- a/solution.py
+++ b/solution.py
@@ -315,8 +315,8 @@
     def kernel(turn_in, top_in, sum_in, part_in, *refs):
         ins = refs[: len(operands)]
         grads = refs[len(operands) : 2 * len(operands)]
-        o_keep, o_send, g_out, r_out, dq_out = refs[2 * len(operands) : -7]
-        s_ref, e_ref, d_ref, kc, vc, kt, vt = refs[-7:]
+        o_keep, o_send, g_out, r_out, kt, d_ref = refs[2 * len(operands) : -5]
+        s_ref, e_ref, kc, vc, vt = refs[-5:]
 
         def body(group, heads):
             put_halves(pairs, sets, ins, group, (kc, vc), (kt, vt))
@@ -355,7 +355,6 @@
             for _, _, at in heads:
                 value_grads[at] = dot(abreast(e_ref, at), twice(cotangents[at][1]), NT)
                 key_grads[at] = dot(abreast(d_ref, at), twice(queries[at]), NT)
-                dq_out[at] = fold_rows(dot(twice(kt[at]), stacked(d_ref, at), NN))
             for pair in group:
                 put_grads(pairs, pair, sets, grads, key_grads, value_grads)
                 both = [output[2 * pair], output[2 * pair + 1]]
@@ -369,16 +368,17 @@
     outs = [struct(*a.shape) for a in operands]
     outs += [struct(pairs, BLOCK, LANES)] * 2
     outs += [struct(heads, HEAD_DIM, BOTH), struct(heads, 1, BOTH)]
-    outs.append(struct(heads, HEAD_DIM, BOTH))
+    outs.append(jax.ShapeDtypeStruct((heads, LANES, total), BF16))
+    outs.append(jax.ShapeDtypeStruct((heads, 2, total, BOTH), BF16))
     return call(
         kernel,
         [turned, tops, sums, partial, *operands],
         outs,
         scratch=[pltpu.VMEM((heads, total, BOTH), F32)]
-        + [pltpu.VMEM((heads, 2, total, BOTH), BF16)] * 2
+        + [pltpu.VMEM((heads, 2, total, BOTH), BF16)]
         + [pltpu.VMEM((heads, total, LANES), BF16)] * 2
-        + [pltpu.VMEM((heads, LANES, total), BF16)] * 2,
-        **costs(pairs, total, 6, 1),
+        + [pltpu.VMEM((heads, LANES, total), BF16)],
+        **costs(pairs, total, 5, 1),
     )
 
 
@@ -394,13 +394,14 @@
             filled += rows
 
 
-def attend_back(pairs, sets, shapes, first, kept, turned, g_scaled, row_dot, dq, last):
+def attend_back(pairs, sets, shapes, first, kept, turned, g_scaled, row_dot, others):
     total = sum(s[3] for s in sets)
     segments = total // BLOCK
 
-    def kernel(turn_in, kt, vc, e_ref, g_in, r_in, dq_in, *refs):
-        grads = refs[: len(shapes)]
-        dq_out = refs[len(shapes) : -1]
+    def kernel(turn_in, kt, vc, e_ref, g_in, r_in, *refs):
+        other_in = refs[: len(others)]
+        grads = refs[len(others) : len(others) + len(shapes)]
+        dq_out = refs[len(others) + len(shapes) : -1]
         d_ref = refs[-1]
         span = pl.ds(first, total)
 
@@ -422,31 +423,34 @@
                 g_rows = cotangents[at]
                 value_grads[at] = dot(abreast(e_ref, at, span), twice(g_rows), NT)
                 key_grads[at] = dot(abreast(d_ref, at), twice(q_rows), NT)
-                part = dot(twice(kt[at, :, span]), stacked(d_ref, at), NN)
-                queries_grad[at] = fold_rows(part) + dq_in[at]
+                if others:
+                    d_lo, kt_hi, d_hi = other_in
+                    part = dot(twice(kt[at, :, span]), stacked(d_ref, at), NN)
+                    part += dot(twice(kt[at, :, total:]), stacked(d_lo, at), NN)
+                    part += dot(twice(kt_hi[at]), stacked(d_hi, at), NN)
+                    queries_grad[at] = fold_rows(part)
             for pair in group:
                 put_grads(pairs, pair, sets, grads, key_grads, value_grads)
-                both = [queries_grad[2 * pair], queries_grad[2 * pair + 1]]
-                if last:
+                if others:
+                    both = [queries_grad[2 * pair], queries_grad[2 * pair + 1]]
                     both = jnp.concatenate(both, axis=0).T * SCALE
                     dq_out[0][pair] = both[:BLOCK]
                     dq_out[1][pair] = both[BLOCK:]
-                else:
-                    for head in range(2):
-                        dq_out[0][2 * pair + head] = both[head]
 
         each_group(pairs, body)
 
     outs = [struct(*shape) for shape in shapes]
-    if last:
+    scratch = []
+    if others:
         outs += [struct(pairs, BLOCK, LANES)] * 2
+        scratch.append(pltpu.VMEM((2 * pairs, 2, total, BOTH), BF16))
     else:
-        outs.append(struct(*dq.shape))
+        outs.append(jax.ShapeDtypeStruct((2 * pairs, 2, total, BOTH), BF16))
     return call(
         kernel,
-        [turned, *kept, g_scaled, row_dot, dq],
+        [turned, *kept, g_scaled, row_dot, *others],
         outs,
-        scratch=[pltpu.VMEM((2 * pairs, 2, total, BOTH), BF16)],
+        scratch=scratch,
         **costs(pairs, total, 4),
     )
 
@@ -489,38 +493,56 @@
 HALF = BLOCK // 2
 
 
-def pack_coarse(pairs, keys, values, scalar):
-    def kernel(bit, k, v, mine, f_theirs, f_mine, c_theirs, c_mine, rest, theirs, sems):
+def pack_theirs(pairs, keys, values, scalar):
+    def kernel(bit, k, v, finest, coarse, rest, block, sems):
         moves = []
-        for out, other in ((theirs, True), (mine, False)):
-            for tile in range(2 * pairs):
-                column = tile % pairs * LANES
-                moves.append((tile // pairs, other, column, out.at[tile]))
+        for tile in range(2 * pairs):
+            moves.append((tile // pairs, True, tile % pairs * LANES, block.at[tile]))
         copies = copy_columns(moves, (k, v), sems, bit[0])
-        for index, copy in enumerate(copies):
+        for tile, copy in enumerate(copies):
             copy.wait()
-            tile = index % (2 * pairs)
-            other = index < 2 * pairs
-            source, finest, coarse = (
-                (theirs, f_theirs, c_theirs) if other else (mine, f_mine, c_mine)
-            )
-            finest[tile] = mean_rows(source, (tile,), 0, HALF, 2)
+            finest[tile] = mean_rows(block, (tile,), 0, HALF, 2)
             coarse[tile] = mean_rows(finest, (tile,), 0, QUARTER, 2)
-            if other:
-                rest[tile, :QUARTER] = half_difference(finest, (tile,), 0, QUARTER)
-                rest[tile, QUARTER:] = half_difference(source, (tile,), 0, HALF)
+            rest[tile, :QUARTER] = half_difference(finest, (tile,), 0, QUARTER)
+            rest[tile, QUARTER:] = half_difference(block, (tile,), 0, HALF)
 
     return call(
         kernel,
         [keys, values],
-        [struct(2 * pairs, BLOCK, LANES)]
-        + [struct(2 * pairs, HALF, LANES)] * 2
-        + [struct(2 * pairs, QUARTER, LANES)] * 2
-        + [struct(2 * pairs, QUARTER + HALF, LANES)],
+        [
+            struct(2 * pairs, HALF, LANES),
+            struct(2 * pairs, QUARTER, LANES),
+            struct(2 * pairs, QUARTER + HALF, LANES),
+        ],
         scratch=[
             pltpu.VMEM((2 * pairs, BLOCK, LANES), F32),
-            pltpu.SemaphoreType.DMA((4 * pairs,)),
+            pltpu.SemaphoreType.DMA((2 * pairs,)),
         ],
+        scalar=scalar,
+        where=pl.ANY,
+    )
+
+
+def pack_mine(pairs, keys, values, scalar):
+    def kernel(bit, k, v, block, finest, coarse, sems):
+        moves = []
+        for tile in range(2 * pairs):
+            moves.append((tile // pairs, False, tile % pairs * LANES, block.at[tile]))
+        copies = copy_columns(moves, (k, v), sems, bit[0])
+        for tile, copy in enumerate(copies):
+            copy.wait()
+            finest[tile] = mean_rows(block, (tile,), 0, HALF, 2)
+            coarse[tile] = mean_rows(finest, (tile,), 0, QUARTER, 2)
+
+    return call(
+        kernel,
+        [keys, values],
+        [
+            struct(2 * pairs, BLOCK, LANES),
+            struct(2 * pairs, HALF, LANES),
+            struct(2 * pairs, QUARTER, LANES),
+        ],
+        scratch=[pltpu.SemaphoreType.DMA((2 * pairs,))],
         scalar=scalar,
         where=pl.ANY,
     )
@@ -802,9 +824,8 @@
         pltpu.with_memory_space_constraint(array, pltpu.HBM)
         for array in (queries, keys, values, cotangent)
     ]
-    mine_kv, f_theirs, f_mine, c_send, c_mine, rest = pack_coarse(
-        pairs, keys, values, scalar
-    )
+    f_theirs, c_send, rest = pack_theirs(pairs, keys, values, scalar)
+    mine_kv, f_mine, c_mine = pack_mine(pairs, keys, values, scalar)
     second = exchange(c_send, 1)
     finest_theirs = exchange(f_theirs, 2)
     coarse = coarsen_pair(lo, pairs, c_mine, second)
@@ -833,11 +854,11 @@
     *kept, tops, sums, partial = attend_first(
         pairs, block_sets + lo_sets, first_in, turned
     )
-    *rs_grads, o_keep, o_send, g_scaled, row_dot, dq = attend_last(
+    *rs_grads, o_keep, o_send, g_scaled, row_dot, kt_hi, d_hi = attend_last(
         pairs, hi_sets, rs, turned, tops, sums, partial
     )
     shapes = [(2 * pairs, *a.shape[1:]) for a in first_in]
-    finest_grad, half_grad, *zs_grads, dq = attend_back(
+    finest_grad, half_grad, *zs_grads, d_lo = attend_back(
         pairs,
         [(level, index - 2, row, rows) for level, index, row, rows in lo_sets],
         shapes[2:],
@@ -846,11 +867,18 @@
         turned,
         g_scaled,
         row_dot,
-        dq,
-        False,
+        [],
     )
     kv_keep, kv_send, dq_keep, dq_send = attend_back(
-        pairs, block_sets, shapes[:2], 0, kept, turned, g_scaled, row_dot, dq, True
+        pairs,
+        block_sets,
+        shapes[:2],
+        0,
+        kept,
+        turned,
+        g_scaled,
+        row_dot,
+        [d_lo, kt_hi, d_hi],
     )
     rough_grads, fine_grads = take_levels(levels, pairs, zs_grads)
     group_grads = hi.scatter(rs_grads)

time: 68.7 us -> 68.8 us (level)
  Pallas kernels: 13.4 us -> 14.7 us
  starting transfers between devices: 31.9 us -> 30.9 us
    pallas_call x16 -> x17, Pallas kernels: 13.4 us -> 14.7 us  [call(): pl.pallas_call(kernel, out_shape=list(outs), in_specs=in_specs, out_specs...]
    ppermute x21, starting transfers between devices: 31.9 us -> 30.9 us  [exchange(): return lax.ppermute(value, AXES, [(i, i ^ offset) for i in range(count)])]
  transfers between devices with their start and end apart: 21 -> 21, of which waited for: 12 -> 11; matrix products, arithmetic and copies ran while one was open for 0% -> 0% of each run, Pallas kernels for 12% -> 14%
where the time goes in v1:
time: 68.8 us; the launch traced here: 68.5 us
  starting transfers between devices  30.9 us (45%)
  waiting for transfers between devices  21.9 us (32%)
  Pallas kernels  14.7 us (21%)
  between operations  0.83 us (1%)
    ppermute x21, starting transfers between devices, exchange(): return lax.ppermute(value, AXES, [(i, i ^ offset) for i in range(count)])  30.9 us
    ppermute x21, waiting for transfers between devices, exchange(): return lax.ppermute(value, AXES, [(i, i ^ offset) for i in range(count)])  21.9 us
    pallas_call x17, Pallas kernels, call(): pl.pallas_call(kernel, out_shape=list(outs), in_specs=in_specs, out_specs...  14.7 us
  transfers between devices with their start and end apart: 21, of which 11 were waited for; matrix products, arithmetic and copies ran while one was open for 0% of the time, Pallas kernels for 14%

profile of v1, /device:TPU:0, one launch (start us, length us, event | category | flops | bytes accessed | tf_op | source)
XLA Modules:
  0.0 68.5 jit_solution(15837134045177788551)
XLA Ops:
  0.6 1.1 %shard_map.91 = (f32[6,64,128]{2,1,0:T(8,128)S(1)}, f32[6,32,128]{2,1,0:T(8,128)S(1)}, f32[6,96,128]{2,1,0:T(8,128)S(1)}) custom-call(s32[1]{0:T(128)} %bitcast.bit, f32[128,768]{1,0:T(8,128)} %k.3, f32[128,768]{1,0:T(8,128)} %v.3), custom_call_target="tpu_custom_call" | custom-call | bytes 1376260 | tf_op jit(solution)/shard_map/pallas_call | solution.py:34
  1.7 3.0 %collective-permute-start.1 = (f32[6,32,128]{2,1,0:T(8,128)S(1)}, f32[6,32,128]{2,1,0:T(8,128)S(1)}, u32[]{:S(2)}, u32[]{:S(2)}) collective-permute-start(f32[6,32,128]{2,1,0:T(8,128)S(1)} %get-tuple-element.131), channel_id=1, source_target_pairs={{0,1},{1,0},{2,3},{3,2},{4,5},{5,4},{6,7},{7,6},{8,9},{9,8},{10,11... | collective-permute-start | bytes 294920 | tf_op jit(solution)/shard_map/ppermute | solution.py:49
  4.8 1.6 %collective-permute-start = (f32[6,64,128]{2,1,0:T(8,128)S(1)}, f32[6,64,128]{2,1,0:T(8,128)S(1)}, u32[]{:S(2)}, u32[]{:S(2)}) collective-permute-start(f32[6,64,128]{2,1,0:T(8,128)S(1)} %get-tuple-element.128), channel_id=1, source_target_pairs={{0,2},{1,3},{2,0},{3,1},{4,6},{5,7},{6,4},{7,5},{8,10},{9,11},{10,... | collective-permute-start | bytes 589832 | tf_op jit(solution)/shard_map/ppermute | solution.py:49
  6.3 1.1 %shard_map.92 = (f32[6,128,128]{2,1,0:T(8,128)S(1)}, f32[6,64,128]{2,1,0:T(8,128)S(1)}, f32[6,32,128]{2,1,0:T(8,128)S(1)}) custom-call(s32[1]{0:T(128)} %bitcast.bit, f32[128,768]{1,0:T(8,128)} %k.3, f32[128,768]{1,0:T(8,128)} %v.3), custom_call_target="tpu_custom_call" | custom-call | bytes 1474564 | tf_op jit(solution)/shard_map/pallas_call | solution.py:34
  7.6 1.9 %collective-permute-start.2 = (f32[6,96,128]{2,1,0:T(8,128)S(1)}, f32[6,96,128]{2,1,0:T(8,128)S(1)}, u32[]{:S(2)}, u32[]{:S(2)}) collective-permute-start(f32[6,96,128]{2,1,0:T(8,128)S(1)} %get-tuple-element.133), channel_id=1, source_target_pairs={{0,1},{1,0},{2,3},{3,2},{4,5},{5,4},{6,7},{7,6},{8,9},{9,8},{10,11... | collective-permute-start | bytes 884744 | tf_op jit(solution)/shard_map/ppermute | solution.py:49
  9.5 2.6 %collective-permute-start.6 = (f32[6,64,128]{2,1,0:T(8,128)S(1)}, f32[6,64,128]{2,1,0:T(8,128)S(1)}, u32[]{:S(2)}, u32[]{:S(2)}) collective-permute-start(f32[6,64,128]{2,1,0:T(8,128)S(1)} %get-tuple-element.132), channel_id=1, source_target_pairs={{0,4},{1,5},{2,6},{3,7},{4,0},{5,1},{6,2},{7,3},{8,12},{9,13},{10,... | collective-permute-start | bytes 589832 | tf_op jit(solution)/shard_map/ppermute | solution.py:49
  12.1 1.6 %collective-permute-start.5 = (f32[6,64,128]{2,1,0:T(8,128)S(1)}, f32[6,64,128]{2,1,0:T(8,128)S(1)}, u32[]{:S(2)}, u32[]{:S(2)}) collective-permute-start(f32[6,64,128]{2,1,0:T(8,128)S(1)} %get-tuple-element.138), channel_id=1, source_target_pairs={{0,2},{1,3},{2,0},{3,1},{4,6},{5,7},{6,4},{7,5},{8,10},{9,11},{10,... | collective-permute-start | bytes 589832 | tf_op jit(solution)/shard_map/ppermute | solution.py:49
  13.6 2.2 %collective-permute-done.2.rest_in = f32[6,96,128]{2,1,0:T(8,128)S(1)} collective-permute-done((f32[6,96,128]{2,1,0:T(8,128)S(1)}, f32[6,96,128]{2,1,0:T(8,128)S(1)}, u32[]{:S(2)}, u32[]{:S(2)}) %collective-permute-start.2) | collective-permute-done | bytes 294944 | tf_op jit(solution)/shard_map/ppermute | solution.py:49
  15.8 1.2 %collective-permute-start.3 = (f32[6,64,128]{2,1,0:T(8,128)S(1)}, f32[6,64,128]{2,1,0:T(8,128)S(1)}, u32[]{:S(2)}, u32[]{:S(2)}) collective-permute-start(f32[6,64,128]{2,1,0:T(8,128)S(1)} %collective-permute-done), channel_id=1, source_target_pairs={{0,1},{1,0},{2,3},{3,2},{4,5},{5,4},{6,7},{7,6},{8,9},{9,8},{10,11... | collective-permute-start | bytes 589832 | tf_op jit(solution)/shard_map/ppermute | solution.py:49
  17.1 1.3 %shard_map.90 = (f32[6,128,128]{2,1,0:T(8,128)S(1)}, f32[6,128,128]{2,1,0:T(8,128)S(1)}) custom-call(s32[1]{0:T(128)} %bitcast.bit, f32[128,768]{1,0:T(8,128)} %one.1, f32[128,768]{1,0:T(8,128)} %two.1), custom_call_target="tpu_custom_call" | custom-call | bytes 1572868 | tf_op jit(solution)/shard_map/pallas_call | solution.py:34
  18.3 1.6 %collective-permute-done.6.refs_5_.refs_3_ = f32[6,64,128]{2,1,0:T(8,128)S(1)} collective-permute-done((f32[6,64,128]{2,1,0:T(8,128)S(1)}, f32[6,64,128]{2,1,0:T(8,128)S(1)}, u32[]{:S(2)}, u32[]{:S(2)}) %collective-permute-start.6) | collective-permute-done | bytes 196640 | tf_op jit(solution)/shard_map/ppermute | solution.py:49
  20.1 1.5 %collective-permute-start.7 = (f32[6,64,128]{2,1,0:T(8,128)S(1)}, f32[6,64,128]{2,1,0:T(8,128)S(1)}, u32[]{:S(2)}, u32[]{:S(2)}) collective-permute-start(f32[6,64,128]{2,1,0:T(8,128)S(1)} %collective-permute-done.6.refs_5_.refs_3_), channel_id=1, source_target_pairs={{0,2},{1,3},{2,0},{3,1},{4,6},{5,7},{6,4},{7,5},{8,10},{9,11},{10,... | collective-permute-start | bytes 589832 | tf_op jit(solution)/shard_map/ppermute | solution.py:49
  21.5 1.2 %collective-permute-start.4 = (f32[6,128,128]{2,1,0:T(8,128)S(1)}, f32[6,128,128]{2,1,0:T(8,128)S(1)}, u32[]{:S(2)}, u32[]{:S(2)}) collective-permute-start(f32[6,128,128]{2,1,0:T(8,128)S(1)} %get-tuple-element.135), channel_id=1, source_target_pairs={{0,1},{1,0},{2,3},{3,2},{4,5},{5,4},{6,7},{7,6},{8,9},{9,8},{10,11... | collective-permute-start | bytes 1179656 | tf_op jit(solution)/shard_map/ppermute | solution.py:49
  22.7 3.0 %collective-permute-done.7.refs_4_.refs_2_ = f32[6,64,128]{2,1,0:T(8,128)S(1)} collective-permute-done((f32[6,64,128]{2,1,0:T(8,128)S(1)}, f32[6,64,128]{2,1,0:T(8,128)S(1)}, u32[]{:S(2)}, u32[]{:S(2)}) %collective-permute-start.7) | collective-permute-done | bytes 196640 | tf_op jit(solution)/shard_map/ppermute | solution.py:49
  25.8 1.6 %collective-permute-start.8 = (f32[6,64,128]{2,1,0:T(8,128)S(1)}, f32[6,64,128]{2,1,0:T(8,128)S(1)}, u32[]{:S(2)}, u32[]{:S(2)}) collective-permute-start(f32[6,64,128]{2,1,0:T(8,128)S(1)} %get-tuple-element.146), channel_id=1, source_target_pairs={{0,16},{1,17},{2,18},{3,19},{4,20},{5,21},{6,22},{7,23},{8,24},{9,... | collective-permute-start | bytes 589832 | tf_op jit(solution)/shard_map/ppermute | solution.py:49
  27.4 4.2 %collective-permute-done.8.refs_1_ = f32[6,64,128]{2,1,0:T(8,128)S(1)} collective-permute-done((f32[6,64,128]{2,1,0:T(8,128)S(1)}, f32[6,64,128]{2,1,0:T(8,128)S(1)}, u32[]{:S(2)}, u32[]{:S(2)}) %collective-permute-start.8) | collective-permute-done | bytes 196640 | tf_op jit(solution)/shard_map/ppermute | solution.py:49
  32.0 2.4 %shard_map.96 = (bf16[6,128,512]{2,1,0:T(8,128)(2,1)S(1)}, bf16[6,512,128]{2,1,0:T(8,128)(2,1)S(1)}, bf16[6,2,512,256]{3,2,1,0:T(8,128)(2,1)S(1)}, f32[6,1,256]{...) custom-call(f32[6,128,256]{2,1,0:T(8,128)S(1)} %shard_map.94.turn_in, ...), custom_call_target="tpu_custom_call" | custom-call | flops 805306368 | bytes 12201984 | tf_op jit(solution)/shard_map/pallas_call | solution.py:34
  34.4 2.5 %shard_map.98 = (f32[6,192,128]{2,1,0:T(8,128)S(1)}, f32[6,64,128]{2,1,0:T(8,128)S(1)}, f32[3,128,128]{2,1,0:T(8,128)S(1)}, f32[3,128,128]{2,1,0:T(8,128)S(1)}, ...) custom-call(f32[6,128,256]{2,1,0:T(8,128)S(1)} %shard_map.94.turn_in, ...), custom_call_target="tpu_custom_call" | custom-call | flops 1006632960 | bytes 7489536 | tf_op jit(solution)/shard_map/pallas_call | solution.py:34
  38.2 1.5 %shard_map.99 = (f32[6,64,128]{2,1,0:T(8,128)S(1)}, f32[6,64,128]{2,1,0:T(8,128)S(1)}, f32[6,64,128]{2,1,0:T(8,128)S(1)}, f32[6,64,128]{2,1,0:T(8,128)S(1)}, bf16[6,2,256,256]{3,2,1,0:T(8,128)(2,1)S(1)}) custom-call(f32[6,128,256]{2,1,0:T(8,128)S(1)} %shard_map.94.turn_in, bf16[6,128,512]{2,1,0:T(8,128)(2,1)S(1)} %get-tuple-element.149.kt, ...), custom_call_target="tpu_custom_call" | custom-call | flops 805306368 | bytes 14555136 | tf_op jit(solution)/shard_map/pallas_call | solution.py:34
  39.9 1.4 %collective-permute-start.12 = (f32[6,96,128]{2,1,0:T(8,128)S(1)}, f32[6,96,128]{2,1,0:T(8,128)S(1)}, u32[]{:S(2)}, u32[]{:S(2)}) collective-permute-start(f32[6,96,128]{2,1,0:T(8,128)S(1)} %pad_maximum_fusion.2), channel_id=1, source_target_pairs={{0,2},{1,3},{2,0},{3,1},{4,6},{5,7},{6,4},{7,5},{8,10},{9,11},{10,... | collective-permute-start | bytes 884744 | tf_op jit(solution)/shard_map/ppermute | solution.py:49
  41.3 1.6 %collective-permute-start.15 = (f32[6,64,128]{2,1,0:T(8,128)S(1)}, f32[6,64,128]{2,1,0:T(8,128)S(1)}, u32[]{:S(2)}, u32[]{:S(2)}) collective-permute-start(f32[6,64,128]{2,1,0:T(8,128)S(1)} %slice_add_fusion), channel_id=1, source_target_pairs={{0,16},{1,17},{2,18},{3,19},{4,20},{5,21},{6,22},{7,23},{8,24},{9,... | collective-permute-start | bytes 589832 | tf_op jit(solution)/shard_map/ppermute | solution.py:49
  42.9 2.2 %shard_map.100 = (f32[6,128,128]{2,1,0:T(8,128)S(1)}, f32[6,128,128]{2,1,0:T(8,128)S(1)}, f32[3,128,128]{2,1,0:T(8,128)S(1)}, f32[3,128,128]{2,1,0:T(8,128)S(1)}) custom-call(f32[6,128,256]{2,1,0:T(8,128)S(1)} %shard_map.94.turn_in, bf16[6,128,512]{2,1,0:T(8,128)(2,1)S(1)} %get-tuple-element.149.kt, bf16[6,512,128]{2,1,0:T(8,128)(2,1)S(1)} %get-tuple-element.150.vc, ...), custom_call_target="tpu_custom_call" | custom-call | flops 805306368 | bytes 18880512 | tf_op jit(solution)/shard_map/pallas_call | solution.py:34
  45.2 1.4 %collective-permute-start.11 = (f32[6,160,128]{2,1,0:T(8,128)S(1)}, f32[6,160,128]{2,1,0:T(8,128)S(1)}, u32[]{:S(2)}, u32[]{:S(2)}) collective-permute-start(f32[6,160,128]{2,1,0:T(8,128)S(1)} %pad_maximum_fusion.1), channel_id=1, source_target_pairs={{0,1},{1,0},{2,3},{3,2},{4,5},{5,4},{6,7},{7,6},{8,9},{9,8},{10,11... | collective-permute-start | bytes 1474568 | tf_op jit(solution)/shard_map/ppermute | solution.py:49
  46.6 1.1 %collective-permute-done.15.refs_1_ = f32[6,64,128]{2,1,0:T(8,128)S(1)} collective-permute-done((f32[6,64,128]{2,1,0:T(8,128)S(1)}, f32[6,64,128]{2,1,0:T(8,128)S(1)}, u32[]{:S(2)}, u32[]{:S(2)}) %collective-permute-start.15) | collective-permute-done | bytes 196640 | tf_op jit(solution)/shard_map/ppermute | solution.py:49
  48.7 2.8 %collective-permute-start.19 = (f32[6,32,128]{2,1,0:T(8,128)S(1)}, f32[6,32,128]{2,1,0:T(8,128)S(1)}, u32[]{:S(2)}, u32[]{:S(2)}) collective-permute-start(f32[6,32,128]{2,1,0:T(8,128)S(1)} %get-tuple-element.188), channel_id=1, source_target_pairs={{0,4},{1,5},{2,6},{3,7},{4,0},{5,1},{6,2},{7,3},{8,12},{9,13},{10,... | collective-permute-start | bytes 294920 | tf_op jit(solution)/shard_map/ppermute | solution.py:49
  51.5 1.6 %collective-permute-start.14 = (f32[6,64,128]{2,1,0:T(8,128)S(1)}, f32[6,64,128]{2,1,0:T(8,128)S(1)}, u32[]{:S(2)}, u32[]{:S(2)}) collective-permute-start(f32[6,64,128]{2,1,0:T(8,128)S(1)} %get-tuple-element.172), channel_id=1, source_target_pairs={{0,1},{1,0},{2,3},{3,2},{4,5},{5,4},{6,7},{7,6},{8,9},{9,8},{10,11... | collective-permute-start | bytes 589832 | tf_op jit(solution)/shard_map/ppermute | solution.py:49
  53.0 3.4 %collective-permute-done.16.refs_0_ = f32[6,64,128]{2,1,0:T(8,128)S(1)} collective-permute-done((f32[6,64,128]{2,1,0:T(8,128)S(1)}, f32[6,64,128]{2,1,0:T(8,128)S(1)}, u32[]{:S(2)}, u32[]{:S(2)}) %collective-permute-start.16) | collective-permute-done | bytes 196640 | tf_op jit(solution)/shard_map/ppermute | solution.py:49
  56.4 1.9 %collective-permute-start.18 = (f32[6,32,128]{2,1,0:T(8,128)S(1)}, f32[6,32,128]{2,1,0:T(8,128)S(1)}, u32[]{:S(2)}, u32[]{:S(2)}) collective-permute-start(f32[6,32,128]{2,1,0:T(8,128)S(1)} %slice_add_fusion.1), channel_id=1, source_target_pairs={{0,4},{1,5},{2,6},{3,7},{4,0},{5,1},{6,2},{7,3},{8,12},{9,13},{10,... | collective-permute-start | bytes 294920 | tf_op jit(solution)/shard_map/ppermute | solution.py:49
  58.3 3.6 %collective-permute-done.14 = f32[6,64,128]{2,1,0:T(8,128)S(1)} collective-permute-done((f32[6,64,128]{2,1,0:T(8,128)S(1)}, f32[6,64,128]{2,1,0:T(8,128)S(1)}, u32[]{:S(2)}, u32[]{:S(2)}) %collective-permute-start.14) | collective-permute-done | bytes 196640 | tf_op jit(solution)/shard_map/ppermute | solution.py:49
  62.6 1.4 %collective-permute-start.20 = (f32[6,32,128]{2,1,0:T(8,128)S(1)}, f32[6,32,128]{2,1,0:T(8,128)S(1)}, u32[]{:S(2)}, u32[]{:S(2)}) collective-permute-start(f32[6,32,128]{2,1,0:T(8,128)S(1)} %get-tuple-element.185), channel_id=1, source_target_pairs={{0,1},{1,0},{2,3},{3,2},{4,5},{5,4},{6,7},{7,6},{8,9},{9,8},{10,11... | collective-permute-start | bytes 294920 | tf_op jit(solution)/shard_map/ppermute | solution.py:49
  65.0 2.6 %collective-permute-done.17.f_theirs = f32[6,64,128]{2,1,0:T(8,128)S(1)} collective-permute-done((f32[6,64,128]{2,1,0:T(8,128)S(1)}, f32[6,64,128]{2,1,0:T(8,128)S(1)}, u32[]{:S(2)}, u32[]{:S(2)}) %collective-permute-start.17) | collective-permute-done | bytes 196640 | tf_op jit(solution)/shard_map/ppermute | solution.py:49
  67.5 1.0 %shard_map.106 = (f32[128,768]{1,0:T(8,128)}, f32[128,768]{1,0:T(8,128)}) custom-call(s32[1]{0:T(128)} %bitcast.bit, f32[6,128,128]{2,1,0:T(8,128)S(1)} %get-tuple-element.165.kept_in, f32[6,96,128]{2,1,0:T(8,128)S(1)} %slice.82.rest_in, f32[6,64,128]{2,1,0:T(8,128)S(1)} %slice.83.f_mine, f32[6,64,128]{2,1,0:T(8,128)S(1)} %collective-permute-done.17.f_theirs, ...), custom_call_target="tpu_custom_call" | custom-call | bytes 2064388 | tf_op jit(solution)/shard_map/pallas_call | solution.py:34
  (36 shorter events, 5.1 us)
Async XLA Ops:
  1.7 5.8 %collective-permute-start.1 = (f32[6,32,128]{2,1,0:T(8,128)S(1)}, f32[6,32,128]{2,1,0:T(8,128)S(1)}, u32[]{:S(2)}, u32[]{:S(2)}) collective-permute-start(f32[6,32,128]{2,1,0:T(8,128)S(1)} %get-tuple-element.131), channel_id=1, source_target_pairs={{0,1},{1,0},{2,3},{3,2},{4,5},{5,4},{6,7},{7,6},{8,9},{9,8},{10,11... | collective-permute-start | bytes 294920 | tf_op jit(solution)/shard_map/ppermute | solution.py:49
  4.8 7.3 %collective-permute-start = (f32[6,64,128]{2,1,0:T(8,128)S(1)}, f32[6,64,128]{2,1,0:T(8,128)S(1)}, u32[]{:S(2)}, u32[]{:S(2)}) collective-permute-start(f32[6,64,128]{2,1,0:T(8,128)S(1)} %get-tuple-element.128), channel_id=1, source_target_pairs={{0,2},{1,3},{2,0},{3,1},{4,6},{5,7},{6,4},{7,5},{8,10},{9,11},{10,... | collective-permute-start | bytes 589832 | tf_op jit(solution)/shard_map/ppermute | solution.py:49
  7.6 8.3 %collective-permute-start.2 = (f32[6,96,128]{2,1,0:T(8,128)S(1)}, f32[6,96,128]{2,1,0:T(8,128)S(1)}, u32[]{:S(2)}, u32[]{:S(2)}) collective-permute-start(f32[6,96,128]{2,1,0:T(8,128)S(1)} %get-tuple-element.133), channel_id=1, source_target_pairs={{0,1},{1,0},{2,3},{3,2},{4,5},{5,4},{6,7},{7,6},{8,9},{9,8},{10,11... | collective-permute-start | bytes 884744 | tf_op jit(solution)/shard_map/ppermute | solution.py:49
  9.5 10.4 %collective-permute-start.6 = (f32[6,64,128]{2,1,0:T(8,128)S(1)}, f32[6,64,128]{2,1,0:T(8,128)S(1)}, u32[]{:S(2)}, u32[]{:S(2)}) collective-permute-start(f32[6,64,128]{2,1,0:T(8,128)S(1)} %get-tuple-element.132), channel_id=1, source_target_pairs={{0,4},{1,5},{2,6},{3,7},{4,0},{5,1},{6,2},{7,3},{8,12},{9,13},{10,... | collective-permute-start | bytes 589832 | tf_op jit(solution)/shard_map/ppermute | solution.py:49
  12.1 8.0 %collective-permute-start.5 = (f32[6,64,128]{2,1,0:T(8,128)S(1)}, f32[6,64,128]{2,1,0:T(8,128)S(1)}, u32[]{:S(2)}, u32[]{:S(2)}) collective-permute-start(f32[6,64,128]{2,1,0:T(8,128)S(1)} %get-tuple-element.138), channel_id=1, source_target_pairs={{0,2},{1,3},{2,0},{3,1},{4,6},{5,7},{6,4},{7,5},{8,10},{9,11},{10,... | collective-permute-start | bytes 589832 | tf_op jit(solution)/shard_map/ppermute | solution.py:49
  15.8 5.7 %collective-permute-start.3 = (f32[6,64,128]{2,1,0:T(8,128)S(1)}, f32[6,64,128]{2,1,0:T(8,128)S(1)}, u32[]{:S(2)}, u32[]{:S(2)}) collective-permute-start(f32[6,64,128]{2,1,0:T(8,128)S(1)} %collective-permute-done), channel_id=1, source_target_pairs={{0,1},{1,0},{2,3},{3,2},{4,5},{5,4},{6,7},{7,6},{8,9},{9,8},{10,11... | collective-permute-start | bytes 589832 | tf_op jit(solution)/shard_map/ppermute | solution.py:49
  20.1 5.7 %collective-permute-start.7 = (f32[6,64,128]{2,1,0:T(8,128)S(1)}, f32[6,64,128]{2,1,0:T(8,128)S(1)}, u32[]{:S(2)}, u32[]{:S(2)}) collective-permute-start(f32[6,64,128]{2,1,0:T(8,128)S(1)} %collective-permute-done.6.refs_5_.refs_3_), channel_id=1, source_target_pairs={{0,2},{1,3},{2,0},{3,1},{4,6},{5,7},{6,4},{7,5},{8,10},{9,11},{10,... | collective-permute-start | bytes 589832 | tf_op jit(solution)/shard_map/ppermute | solution.py:49
  21.5 10.1 %collective-permute-start.4 = (f32[6,128,128]{2,1,0:T(8,128)S(1)}, f32[6,128,128]{2,1,0:T(8,128)S(1)}, u32[]{:S(2)}, u32[]{:S(2)}) collective-permute-start(f32[6,128,128]{2,1,0:T(8,128)S(1)} %get-tuple-element.135), channel_id=1, source_target_pairs={{0,1},{1,0},{2,3},{3,2},{4,5},{5,4},{6,7},{7,6},{8,9},{9,8},{10,11... | collective-permute-start | bytes 1179656 | tf_op jit(solution)/shard_map/ppermute | solution.py:49
  25.8 5.7 %collective-permute-start.8 = (f32[6,64,128]{2,1,0:T(8,128)S(1)}, f32[6,64,128]{2,1,0:T(8,128)S(1)}, u32[]{:S(2)}, u32[]{:S(2)}) collective-permute-start(f32[6,64,128]{2,1,0:T(8,128)S(1)} %get-tuple-element.146), channel_id=1, source_target_pairs={{0,16},{1,17},{2,18},{3,19},{4,20},{5,21},{6,22},{7,23},{8,24},{9,... | collective-permute-start | bytes 589832 | tf_op jit(solution)/shard_map/ppermute | solution.py:49
  31.9 2.5 %collective-permute-start.9 = (f32[6,192,128]{2,1,0:T(8,128)S(1)}, f32[6,192,128]{2,1,0:T(8,128)S(1)}, u32[]{:S(2)}, u32[]{:S(2)}) collective-permute-start(f32[6,192,128]{2,1,0:T(8,128)S(1)} %pad_maximum_fusion), channel_id=1, source_target_pairs={{0,8},{1,9},{2,10},{3,11},{4,12},{5,13},{6,14},{7,15},{8,0},{9,1},... | collective-permute-start | bytes 1769480 | tf_op jit(solution)/shard_map/ppermute | solution.py:49
  36.9 4.4 %collective-permute-start.13 = (f32[6,192,128]{2,1,0:T(8,128)S(1)}, f32[6,192,128]{2,1,0:T(8,128)S(1)}, u32[]{:S(2)}, u32[]{:S(2)}) collective-permute-start(f32[6,192,128]{2,1,0:T(8,128)S(1)} %get-tuple-element.171), channel_id=1, source_target_pairs={{0,8},{1,9},{2,10},{3,11},{4,12},{5,13},{6,14},{7,15},{8,0},{9,1},... | collective-permute-start | bytes 1769480 | tf_op jit(solution)/shard_map/ppermute | solution.py:49
  37.5 7.7 %collective-permute-start.10 = (f32[3,128,128]{2,1,0:T(8,128)S(1)}, f32[3,128,128]{2,1,0:T(8,128)S(1)}, u32[]{:S(2)}, u32[]{:S(2)}) collective-permute-start(f32[3,128,128]{2,1,0:T(8,128)S(1)} %get-tuple-element.158), channel_id=1, source_target_pairs={{0,1},{1,0},{2,3},{3,2},{4,5},{5,4},{6,7},{7,6},{8,9},{9,8},{10,11... | collective-permute-start | bytes 589832 | tf_op jit(solution)/shard_map/ppermute | solution.py:49
  39.9 8.8 %collective-permute-start.12 = (f32[6,96,128]{2,1,0:T(8,128)S(1)}, f32[6,96,128]{2,1,0:T(8,128)S(1)}, u32[]{:S(2)}, u32[]{:S(2)}) collective-permute-start(f32[6,96,128]{2,1,0:T(8,128)S(1)} %pad_maximum_fusion.2), channel_id=1, source_target_pairs={{0,2},{1,3},{2,0},{3,1},{4,6},{5,7},{6,4},{7,5},{8,10},{9,11},{10,... | collective-permute-start | bytes 884744 | tf_op jit(solution)/shard_map/ppermute | solution.py:49
  41.3 6.4 %collective-permute-start.15 = (f32[6,64,128]{2,1,0:T(8,128)S(1)}, f32[6,64,128]{2,1,0:T(8,128)S(1)}, u32[]{:S(2)}, u32[]{:S(2)}) collective-permute-start(f32[6,64,128]{2,1,0:T(8,128)S(1)} %slice_add_fusion), channel_id=1, source_target_pairs={{0,16},{1,17},{2,18},{3,19},{4,20},{5,21},{6,22},{7,23},{8,24},{9,... | collective-permute-start | bytes 589832 | tf_op jit(solution)/shard_map/ppermute | solution.py:49
  45.2 17.2 %collective-permute-start.11 = (f32[6,160,128]{2,1,0:T(8,128)S(1)}, f32[6,160,128]{2,1,0:T(8,128)S(1)}, u32[]{:S(2)}, u32[]{:S(2)}) collective-permute-start(f32[6,160,128]{2,1,0:T(8,128)S(1)} %pad_maximum_fusion.1), channel_id=1, source_target_pairs={{0,1},{1,0},{2,3},{3,2},{4,5},{5,4},{6,7},{7,6},{8,9},{9,8},{10,11... | collective-permute-start | bytes 1474568 | tf_op jit(solution)/shard_map/ppermute | solution.py:49
  47.8 8.6 %collective-permute-start.16 = (f32[6,64,128]{2,1,0:T(8,128)S(1)}, f32[6,64,128]{2,1,0:T(8,128)S(1)}, u32[]{:S(2)}, u32[]{:S(2)}) collective-permute-start(f32[6,64,128]{2,1,0:T(8,128)S(1)} %get-tuple-element.177), channel_id=1, source_target_pairs={{0,2},{1,3},{2,0},{3,1},{4,6},{5,7},{6,4},{7,5},{8,10},{9,11},{10,... | collective-permute-start | bytes 589832 | tf_op jit(solution)/shard_map/ppermute | solution.py:49
  48.7 13.8 %collective-permute-start.19 = (f32[6,32,128]{2,1,0:T(8,128)S(1)}, f32[6,32,128]{2,1,0:T(8,128)S(1)}, u32[]{:S(2)}, u32[]{:S(2)}) collective-permute-start(f32[6,32,128]{2,1,0:T(8,128)S(1)} %get-tuple-element.188), channel_id=1, source_target_pairs={{0,4},{1,5},{2,6},{3,7},{4,0},{5,1},{6,2},{7,3},{8,12},{9,13},{10,... | collective-permute-start | bytes 294920 | tf_op jit(solution)/shard_map/ppermute | solution.py:49
  51.5 10.4 %collective-permute-start.14 = (f32[6,64,128]{2,1,0:T(8,128)S(1)}, f32[6,64,128]{2,1,0:T(8,128)S(1)}, u32[]{:S(2)}, u32[]{:S(2)}) collective-permute-start(f32[6,64,128]{2,1,0:T(8,128)S(1)} %get-tuple-element.172), channel_id=1, source_target_pairs={{0,1},{1,0},{2,3},{3,2},{4,5},{5,4},{6,7},{7,6},{8,9},{9,8},{10,11... | collective-permute-start | bytes 589832 | tf_op jit(solution)/shard_map/ppermute | solution.py:49
  56.4 6.1 %collective-permute-start.18 = (f32[6,32,128]{2,1,0:T(8,128)S(1)}, f32[6,32,128]{2,1,0:T(8,128)S(1)}, u32[]{:S(2)}, u32[]{:S(2)}) collective-permute-start(f32[6,32,128]{2,1,0:T(8,128)S(1)} %slice_add_fusion.1), channel_id=1, source_target_pairs={{0,4},{1,5},{2,6},{3,7},{4,0},{5,1},{6,2},{7,3},{8,12},{9,13},{10,... | collective-permute-start | bytes 294920 | tf_op jit(solution)/shard_map/ppermute | solution.py:49
  61.9 5.7 %collective-permute-start.17 = (f32[6,64,128]{2,1,0:T(8,128)S(1)}, f32[6,64,128]{2,1,0:T(8,128)S(1)}, u32[]{:S(2)}, u32[]{:S(2)}) collective-permute-start(f32[6,64,128]{2,1,0:T(8,128)S(1)} %collective-permute-done.14), channel_id=1, source_target_pairs={{0,2},{1,3},{2,0},{3,1},{4,6},{5,7},{6,4},{7,5},{8,10},{9,11},{10,... | collective-permute-start | bytes 589832 | tf_op jit(solution)/shard_map/ppermute | solution.py:49
  62.6 5.0 %collective-permute-start.20 = (f32[6,32,128]{2,1,0:T(8,128)S(1)}, f32[6,32,128]{2,1,0:T(8,128)S(1)}, u32[]{:S(2)}, u32[]{:S(2)}) collective-permute-start(f32[6,32,128]{2,1,0:T(8,128)S(1)} %get-tuple-element.185), channel_id=1, source_target_pairs={{0,1},{1,0},{2,3},{3,2},{4,5},{5,4},{6,7},{7,6},{8,9},{9,8},{10,11... | collective-permute-start | bytes 294920 | tf_op jit(solution)/shard_map/ppermute | solution.py:49
